TPU v7x, 128 devices: a whole 4x4x4 slice. The times are simulated.
128 devices in a mesh: dp: 128 (over y, z, x, core).
Axes of the slice: x: 4, y: 4, z: 4, core: 2. Of those that a mesh axis runs over, the one named last changes fastest.
Arguments:
- grads: bfloat16 [1152, 7168], P('dp'), may hold values from -60 to 60
- momentum_slots: float32 [384, 56, 1152], P('dp'), may hold values from -60 to 60
- table: int32 [128], replicated, may hold values from 0 to 127, as said below
Outputs:
- update: bfloat16 [1152, 7168], replicated
- new_momentum: float32 [384, 56, 1152], P('dp')
Inputs may be any that keep to these rules, and one draw needn't show every extreme that they name: `table`: no device owns more than 3 blocks, and some device owns exactly 3.
All inputs are finite; a program needn't handle non-finite values.
Results may differ from a plain program's by a relative error of at most 0.001.
Values may be sent and summed in bfloat16 or wider, within the bound.
A program may use at most 512 MiB of HBM per device.

v0:
```python
import math

import jax
import jax.numpy as jnp
from jax import lax
from jax.sharding import PartitionSpec as P

R = 576
C = 7168
ITERS = 5


coef_a = 3.4445
coef_b = -4.775
coef_c = 2.0315
epsilon = 1e-07


def slot_of_blocks(table, slot_count):
    positions = jnp.arange(table.shape[0], dtype=jnp.int32)
    matching = (table[None, :] == table[:, None]) & (positions[None, :] < positions[:, None])
    ranking = jnp.sum(matching.astype(jnp.int32), axis=1)
    return table * slot_count + ranking


def gram_sum(values):
    partial_gram = jnp.einsum("jcmr,jcms->mrs", values, values, precision=lax.Precision.HIGHEST)
    return lax.psum(partial_gram, "dp")


def quintic(gram_mat):
    squared = jnp.matmul(gram_mat, gram_mat, precision=lax.Precision.HIGHEST)
    return coef_b * gram_mat + coef_c * squared


def apply_poly(values, poly_mat):
    return jnp.einsum("jcms,mrs->jcmr", values, poly_mat, precision=lax.Precision.HIGHEST)


def local(grads, momentum_slots, table):
    devices = lax.axis_size("dp")
    my_index = lax.axis_index("dp")
    row_dev = grads.shape[0]
    full_width = grads.shape[1]
    slot_count = momentum_slots.shape[0]
    block_width = momentum_slots.shape[1]
    rows_all = momentum_slots.shape[2]
    block_total = full_width // block_width
    layers = rows_all // R
    slots_all = devices * slot_count
    slot_index = slot_of_blocks(table, slot_count)
    hits = slot_index[None, :] == jnp.arange(slots_all, dtype=jnp.int32)[:, None]
    occupied = jnp.any(hits, axis=1)
    block_of = jnp.sum(
        jnp.where(hits, jnp.arange(block_total, dtype=jnp.int32)[None, :], 0), axis=1
    )
    pieces = grads.reshape(row_dev, block_total, block_width).transpose(1, 2, 0)
    outgoing = jnp.take(pieces, block_of, axis=0) * occupied[:, None, None].astype(jnp.bfloat16)
    outgoing = outgoing.reshape(devices, slot_count, block_width, row_dev)
    arrived = lax.all_to_all(outgoing, "dp", split_axis=0, concat_axis=3, tiled=True)
    arrived = arrived.reshape(slot_count, block_width, rows_all)
    mine = lax.dynamic_slice_in_dim(occupied, my_index * slot_count, slot_count)
    refreshed = (0.95 * momentum_slots + arrived.astype(jnp.float32)) * mine[:, None, None].astype(
        jnp.float32
    )
    per_layer = refreshed.reshape(slot_count, block_width, layers, R)
    squares = lax.psum(jnp.sum(per_layer * per_layer, axis=(0, 1, 3)), "dp")
    frob_norm = jnp.sqrt(squares)
    current = per_layer / (frob_norm + epsilon)[None, None, :, None]
    for sweep in range(ITERS):
        poly_mat = quintic(gram_sum(current))
        current = coef_a * current + apply_poly(current, poly_mat)
    rms_factor = 0.2 * math.sqrt(max(R, C))
    scaled = (rms_factor * current).reshape(slot_count, block_width, rows_all).astype(jnp.bfloat16)
    going_back = scaled.reshape(slot_count, block_width, devices, row_dev)
    returned = lax.all_to_all(going_back, "dp", split_axis=2, concat_axis=0, tiled=True)
    returned = returned.reshape(slots_all, block_width, row_dev)
    ordered = jnp.take(returned, slot_index, axis=0).transpose(2, 0, 1).reshape(row_dev, full_width)
    update = lax.all_gather(ordered, "dp", axis=0, tiled=True)
    return (update, refreshed)


def solution(mesh):
    in_specs = (P("dp", None), P("dp", None, None), P())
    out_specs = (P(), P("dp", None, None))
    return jax.shard_map(local, mesh=mesh, in_specs=in_specs, out_specs=out_specs, check_vma=False)
```

profile of v0, /device:TPU:1, one launch (start us, length us, event | category | flops | bytes accessed | tf_op | source)
XLA Modules:
  0.0 1109.7 jit_solution(4619782626221269335)
XLA Ops:
  7.2 0.9 convert_reduce_fusion
  8.1 0.7 compare_and_fusion.1
  9.6 1.5 reshape.70
  11.3 1.9 gather_fusion
  13.2 0.8 copy_bitcast_fusion.1
  14.0 1.9 reshape.113
  15.9 11.5 %all-to-all-start = ((bf16[128,2,756]{2,1,0:T(2,128)(2,1)}), bf16[128,2,756]{2,1,0:T(2,128)(2,1)S(1)}, u32[]{:S(2)}, u32[]{:S(2)}) async-start(bf16[128,2,756]{2,1,0:T(2,128)(2,1)} %reshape.113), calls=%async_computation | async-start | bytes 786432 | tf_op jit(solution)/shard_map/all_to_all | solution.py:60
  27.6 12.2 %all-to-all-done = bf16[128,2,756]{2,1,0:T(2,128)(2,1)S(1)} async-done(((bf16[128,2,756]{2,1,0:T(2,128)(2,1)}), bf16[128,2,756]{2,1,0:T(2,128)(2,1)S(1)}, u32[]{:S(2)}, u32[]{:S(2)}) %all-to-all-start) | async-done | bytes 387104 | tf_op jit(solution)/shard_map/all_to_all | solution.py:60
  39.8 0.8 reshape.114
  40.5 0.3 bitcast_convert_fusion
  40.8 1.9 copy.44
  42.7 1.5 multiply_reduce_fusion
  44.5 62.9 %psum.42 = f32[2]{0:T(128)S(1)} all-reduce(f32[2]{0:T(128)S(1)} %reduce_sum.44), channel_id=1, replica_groups=mesh['dp'=128] {'dp'}, use_global_device_ids=true, to_apply=%region_5.6 | all-reduce | flops 2 | bytes 16 | tf_op jit(solution)/shard_map/psum | solution.py:67
  107.4 0.6 reshape.71
  108.1 4.6 convolution_bitcast_fusion.4
  112.8 0.3 all-reduce.8.cloned.1.call-start
  113.1 148.3 %all-reduce.6.cloned.1.call-done = f32[2,576,576]{2,1,0:T(8,128)} async-done(((f32[2,576,576]{2,1,0:T(8,128)}), f32[2,576,576]{2,1,0:T(8,128)}) %all-reduce.6.cloned.1.call-update) | async-done | bytes 2654224 | tf_op jit(solution)/shard_map/psum | solution.py:28
  261.4 11.0 fusion.44
  272.5 3.8 fusion.16
  276.5 4.7 convolution_bitcast_fusion.3
  281.2 0.4 all-reduce.10.cloned.1.call-start
  281.7 150.0 %all-reduce.8.cloned.1.call-done = f32[2,576,576]{2,1,0:T(8,128)} async-done(((f32[2,576,576]{2,1,0:T(8,128)}), f32[2,576,576]{2,1,0:T(8,128)}) %all-reduce.8.cloned.1.call-update) | async-done | bytes 2654224 | tf_op jit(solution)/shard_map/psum | solution.py:28
  431.7 11.0 fusion.45
  442.7 3.8 fusion.12
  446.7 4.6 convolution_bitcast_fusion.2
  451.6 150.3 %all-reduce.10.cloned.1.call-done = f32[2,576,576]{2,1,0:T(8,128)} async-done(((f32[2,576,576]{2,1,0:T(8,128)}), f32[2,576,576]{2,1,0:T(8,128)}) %all-reduce.10.cloned.1.call-update) | async-done | bytes 2654224 | tf_op jit(solution)/shard_map/psum | solution.py:28
  601.9 11.0 fusion.46
  612.9 3.8 fusion.8
  616.9 4.8 convolution_bitcast_fusion.1
  621.6 0.3 all-reduce.14.cloned.1.call-start
  621.9 150.2 %all-reduce.12.cloned.1.call-done = f32[2,576,576]{2,1,0:T(8,128)} async-done(((f32[2,576,576]{2,1,0:T(8,128)}), f32[2,576,576]{2,1,0:T(8,128)}) %all-reduce.12.cloned.1.call-update) | async-done | bytes 2654224 | tf_op jit(solution)/shard_map/psum | solution.py:28
  772.1 11.0 fusion.47
  783.2 3.8 fusion.4
  787.1 4.6 convolution_bitcast_fusion
  791.8 150.4 %all-reduce.14.cloned.1.call-done = f32[2,576,576]{2,1,0:T(8,128)} async-done(((f32[2,576,576]{2,1,0:T(8,128)}), f32[2,576,576]{2,1,0:T(8,128)}) %all-reduce.14.cloned.1.call-update) | async-done | bytes 2654224 | tf_op jit(solution)/shard_map/psum | solution.py:28
  942.2 11.3 %fusion.48 = f32[2,576,576]{2,1,0:T(8,128)S(1)} fusion(f32[2,576,576]{2,1,0:T(8,128)} %all-reduce.14.cloned.1.call-done), kind=kOutput, calls=%fused_computation.83 | convolution fusion | flops 4586471424 | bytes 5308416 | tf_op jit(solution)/shard_map/dot_general | solution.py:32
  953.5 3.8 fusion
  957.5 0.8 copy.46
  958.2 1.9 reshape.115
  960.1 6.6 all-to-all-start.1
  966.8 12.2 %all-to-all-done.1 = bf16[128,2,756]{2,1,0:T(2,128)(2,1)S(1)} async-done(((bf16[128,2,756]{2,1,0:T(2,128)(2,1)}), bf16[128,2,756]{2,1,0:T(2,128)(2,1)S(1)}, u32[]{:S(2)}, u32[]{:S(2)}) %all-to-all-start.1) | async-done | bytes 387104 | tf_op jit(solution)/shard_map/all_to_all | solution.py:76
  979.0 0.8 reshape.116
  979.8 0.4 bitcast_bitcast_fusion
  980.2 0.3 copy.56
  980.5 0.7 gather_fusion.1
  981.5 1.2 reshape.94
  982.8 96.8 %all-gather.3.cloned.1.call-done = bf16[128,9,7168]{2,1,0:T(8,128)(2,1)} async-done(((bf16[1,9,7168]{2,1,0:T(8,128)(2,1)}), bf16[128,9,7168]{2,1,0:T(8,128)(2,1)}) %all-gather.3.cloned.1.call-update) | async-done | bytes 16515088 | tf_op jit(solution)/shard_map/all_gather | solution.py:79
  1079.5 22.9 %reshape.95 = bf16[1152,7168]{1,0:T(8,128)(2,1)} reshape(bf16[128,9,7168]{2,1,0:T(8,128)(2,1)} %all-gather.3.cloned.1.call-done) | data formatting | bytes 33030144
  (44 shorter events, 2.8 us)
Async XLA Ops:
  15.9 23.8 %all-to-all-start = ((bf16[128,2,756]{2,1,0:T(2,128)(2,1)}), bf16[128,2,756]{2,1,0:T(2,128)(2,1)S(1)}, u32[]{:S(2)}, u32[]{:S(2)}) async-start(bf16[128,2,756]{2,1,0:T(2,128)(2,1)} %reshape.113), calls=%async_computation | async-start | bytes 786432 | tf_op jit(solution)/shard_map/all_to_all | solution.py:60
  27.4 234.0 %all-reduce.6.cloned.1.call-start = ((), (), s32[]{:S(2)}) async-start(), calls=%async_computation.2 | async-start | bytes 5898240 | tf_op jit(solution)/shard_map/psum | solution.py:28
  44.3 68.5 %copy-start.5 = (f32[3,56,1152]{2,1,0:T(8,128)}, f32[3,56,1152]{2,1,0:T(8,128)S(1)}, u32[]{:S(2)}) copy-start(f32[3,56,1152]{2,1,0:T(8,128)S(1)} %get-tuple-element.11) | copy-start | bytes 2322436
  112.8 318.9 %all-reduce.8.cloned.1.call-start = ((), (), s32[]{:S(2)}) async-start(), calls=%async_computation.3 | async-start | bytes 5898240 | tf_op jit(solution)/shard_map/psum | solution.py:28
  261.4 11.1 copy-start
  281.2 320.6 %all-reduce.10.cloned.1.call-start = ((), (), s32[]{:S(2)}) async-start(), calls=%async_computation.4 | async-start | bytes 5898240 | tf_op jit(solution)/shard_map/psum | solution.py:28
  431.7 11.1 copy-start.1
  451.4 320.7 %all-reduce.12.cloned.1.call-start = ((), (), s32[]{:S(2)}) async-start(), calls=%async_computation.5 | async-start | bytes 5898240 | tf_op jit(solution)/shard_map/psum | solution.py:28
  601.9 11.1 copy-start.2
  621.6 320.6 %all-reduce.14.cloned.1.call-start = ((), (), s32[]{:S(2)}) async-start(), calls=%async_computation.6 | async-start | bytes 5898240 | tf_op jit(solution)/shard_map/psum | solution.py:28
  772.1 11.1 copy-start.3
  942.2 11.3 %copy-start.4 = (f32[2,576,576]{2,1,0:T(8,128)S(1)}, f32[2,576,576]{2,1,0:T(8,128)}, u32[]{:S(2)}) copy-start(f32[2,576,576]{2,1,0:T(8,128)} %all-reduce.14.cloned.1.call-done) | copy-start | bytes 7962628
  960.1 18.9 %all-to-all-start.1 = ((bf16[128,2,756]{2,1,0:T(2,128)(2,1)}), bf16[128,2,756]{2,1,0:T(2,128)(2,1)S(1)}, u32[]{:S(2)}, u32[]{:S(2)}) async-start(bf16[128,2,756]{2,1,0:T(2,128)(2,1)} %reshape.115), calls=%async_computation.1 | async-start | bytes 786432 | tf_op jit(solution)/shard_map/all_to_all | solution.py:76
  966.7 112.8 %all-gather.3.cloned.1.call-start = ((), (), s32[]{:S(2)}) async-start(), calls=%async_computation.7 | async-start | bytes 29589504 | tf_op jit(solution)/shard_map/all_gather | solution.py:79
Sparse Core Ops, SparseCore 0:
  112.9 148.4 all-reduce.5
  281.4 150.2 all-reduce.7
  451.5 150.3 all-reduce.9
  621.8 150.2 all-reduce.11
  791.9 150.2 all-reduce.13
  982.9 96.6 all-gather.2
where the time goes:
time: 1120 us; the launch traced here: 1110 us
  waiting for transfers between devices  870 us (78%)
  matrix products  98 us (9%)
  blocking collectives  62.9 us (6%)
  local copies, waits for them, and re-layouts  38.2 us (3%)
  starting transfers between devices  19.3 us (2%)
  between operations  14.9 us (1%)
    psum x5, waiting for transfers between devices, gram_sum(): return lax.psum(partial_gram, 'dp')  749 us
    all_gather x1, waiting for transfers between devices, local(): update = lax.all_gather(ordered, 'dp', axis=0, tiled=True)  96.8 us
    psum x1, blocking collectives, local(): squares = lax.psum(jnp.sum(per_layer * per_layer, axis=(0, 1, 3)), 'dp')  62.9 us
    dot_general x5, matrix products, quintic(): squared = jnp.matmul(gram_mat, gram_mat, precision=lax.Precision.HIGHEST)  55.5 us
    unnamed x18, local copies, waits for them, and re-layouts  29.3 us
    dot_general x5, matrix products, gram_sum(): jnp.einsum('jcmr,jcms->mrs', values, values, precision=lax.Precision.HIGH...  23.4 us
  transfers between devices with their start and end apart: 8, of which 8 were waited for; matrix products, arithmetic and copies ran while one was open for 0% of the time, Pallas kernels for 0%

commit v1 on v0

--- a/solution.py
+++ b/solution.py
@@ -64,12 +64,18 @@
         jnp.float32
     )
     per_layer = refreshed.reshape(slot_count, block_width, layers, R)
-    squares = lax.psum(jnp.sum(per_layer * per_layer, axis=(0, 1, 3)), "dp")
-    frob_norm = jnp.sqrt(squares)
-    current = per_layer / (frob_norm + epsilon)[None, None, :, None]
+    gram_raw = gram_sum(per_layer)
+    frob_norm = jnp.sqrt(jnp.trace(gram_raw, axis1=1, axis2=2))
+    inverse = 1.0 / (frob_norm + epsilon)
+    gram_mat = gram_raw * (inverse * inverse)[:, None, None]
+    eye = jnp.eye(R, dtype=jnp.float32)
+    current = per_layer * inverse[None, None, :, None]
     for sweep in range(ITERS):
-        poly_mat = quintic(gram_sum(current))
-        current = coef_a * current + apply_poly(current, poly_mat)
+        poly_mat = coef_a * eye + quintic(gram_mat)
+        current = apply_poly(current, poly_mat)
+        if sweep < ITERS - 1:
+            half = jnp.matmul(poly_mat, gram_mat, precision=lax.Precision.HIGHEST)
+            gram_mat = jnp.matmul(half, poly_mat, precision=lax.Precision.HIGHEST)
     rms_factor = 0.2 * math.sqrt(max(R, C))
     scaled = (rms_factor * current).reshape(slot_count, block_width, rows_all).astype(jnp.bfloat16)
     going_back = scaled.reshape(slot_count, block_width, devices, row_dev)

time: 1120 us -> 493 us (0.44)
  waiting for transfers between devices: 870 us -> 269 us
  blocking collectives: 62.9 us -> 0 us
  matrix products: 98 us -> 140 us
    psum x5 -> x1, waiting for transfers between devices: 749 us -> 148 us  [gram_sum(): return lax.psum(partial_gram, 'dp')]
    dot_general x0 -> x8, matrix products: none -> 71.6 us  [the longest x4 36 us: local(): gram_mat = jnp.matmul(half, poly_mat, precision=lax.Precision.HIGHEST)]
    psum x1 -> x0, blocking collectives: 62.9 us -> none  [local(): squares = lax.psum(jnp.sum(per_layer * per_layer, axis=(0, 1, 3)), 'dp')]
    dot_general x5 -> x1, matrix products: 23.4 us -> 4.65 us  [gram_sum(): jnp.einsum('jcmr,jcms->mrs', values, values, precision=lax.Precision.HIGH...]
    dot_general x5, matrix products: 55.5 us -> 43.5 us  [quintic(): squared = jnp.matmul(gram_mat, gram_mat, precision=lax.Precision.HIGHEST)]
    unnamed x18 -> x10, local copies, waits for them, and re-layouts: 29.3 us -> 29.3 us
  transfers between devices with their start and end apart: 8 -> 4, of which waited for: 8 -> 4; matrix products, arithmetic and copies ran while one was open for 0% -> 0% of each run, Pallas kernels for 0% -> 0%
where the time goes in v1:
time: 493 us; the launch traced here: 488 us
  waiting for transfers between devices  269 us (55%)
  matrix products  140 us (28%)
  local copies, waits for them, and re-layouts  37.7 us (8%)
  starting transfers between devices  18.2 us (4%)
  between operations  14.8 us (3%)
  other arithmetic  7.6 us (2%)
    psum x1, waiting for transfers between devices, gram_sum(): return lax.psum(partial_gram, 'dp')  148 us
    all_gather x1, waiting for transfers between devices, local(): update = lax.all_gather(ordered, 'dp', axis=0, tiled=True)  96.8 us
    dot_general x5, matrix products, quintic(): squared = jnp.matmul(gram_mat, gram_mat, precision=lax.Precision.HIGHEST)  43.5 us
    dot_general x4, matrix products, local(): gram_mat = jnp.matmul(half, poly_mat, precision=lax.Precision.HIGHEST)  36 us
    dot_general x4, matrix products, local(): half = jnp.matmul(poly_mat, gram_mat, precision=lax.Precision.HIGHEST)  35.5 us
    unnamed x10, local copies, waits for them, and re-layouts  29.3 us
    unnamed x5, matrix products  20.7 us
    all_to_all x1, waiting for transfers between devices, local(): lax.all_to_all(going_back, 'dp', split_axis=2, concat_axis=0, tiled=True)  12.2 us
  transfers between devices with their start and end apart: 4, of which 4 were waited for; matrix products, arithmetic and copies ran while one was open for 0% of the time, Pallas kernels for 0%

profile of v1, /device:TPU:1, one launch (start us, length us, event | category | flops | bytes accessed | tf_op | source)
XLA Modules:
  0.0 488.2 jit_solution(4584379083599064882)
XLA Ops:
  7.2 0.9 convert_reduce_fusion
  8.1 0.7 compare_and_fusion.1
  9.3 0.2 reshape.91
  9.6 1.5 reshape.87
  11.0 0.2 copy.69
  11.3 1.9 gather_fusion
  13.2 0.8 copy_bitcast_fusion.1
  14.0 1.9 reshape.126
  15.9 11.5 %all-to-all-start = ((bf16[128,2,756]{2,1,0:T(2,128)(2,1)}), bf16[128,2,756]{2,1,0:T(2,128)(2,1)S(1)}, u32[]{:S(2)}, u32[]{:S(2)}) async-start(bf16[128,2,756]{2,1,0:T(2,128)(2,1)} %reshape.126), calls=%async_computation | async-start | bytes 786432 | tf_op jit(solution)/shard_map/all_to_all | solution.py:60
  27.6 12.2 %all-to-all-done = bf16[128,2,756]{2,1,0:T(2,128)(2,1)S(1)} async-done(((bf16[128,2,756]{2,1,0:T(2,128)(2,1)}), bf16[128,2,756]{2,1,0:T(2,128)(2,1)S(1)}, u32[]{:S(2)}, u32[]{:S(2)}) %all-to-all-start) | async-done | bytes 387104 | tf_op jit(solution)/shard_map/all_to_all | solution.py:60
  39.8 0.8 reshape.127
  40.5 0.3 bitcast_convert_fusion
  40.8 1.5 copy.48
  42.3 1.3 add_multiply_fusion
  43.6 0.6 reshape.88
  44.2 4.6 convolution_bitcast_fusion
  49.1 148.1 %all-reduce.2.cloned.1.call-done = f32[2,576,576]{2,1,0:T(8,128)} async-done(((f32[2,576,576]{2,1,0:T(8,128)}), f32[2,576,576]{2,1,0:T(8,128)}) %all-reduce.2.cloned.1.call-update) | async-done | bytes 2654224 | tf_op jit(solution)/shard_map/psum | solution.py:28
  197.3 2.6 select_reduce_fusion
  200.0 9.1 %fusion.31 = f32[2,576,576]{2,1,0:T(8,128)S(1)} fusion(f32[2,576,576]{2,1,0:T(8,128)S(1)} %copy-done, f32[2]{0:T(128)S(1)} %get-tuple-element.10), kind=kOutput, calls=%fused_computation.38 | convolution fusion | flops 4587134976 | bytes 5308424 | tf_op jit(solution)/shard_map/dot_general | solution.py:32
  209.1 9.0 %fusion.25 = f32[2,576,576]{2,1,0:T(8,128)S(1)} fusion(f32[2,576,576]{2,1,0:T(8,128)S(1)} %fusion.31, f32[2,576,576]{2,1,0:T(8,128)S(1)} %copy-done, f32[2]{0:T(128)S(1)} %get-tuple-element.10, f32[576,576]{1,0:T(8,128)S(1)} %broadcast_select_fusion), kind=kOutput, calls=%fused_computation.31 | convolution fusion | flops 4590452736 | bytes 9289736 | tf_op jit(solution)/shard_map/dot_general | solution.py:77
  218.1 9.2 %fusion.24 = f32[2,576,576]{2,1,0:T(8,128)S(1)} fusion(f32[2,576,576]{2,1,0:T(8,128)S(1)} %fusion.25, f32[2,576,576]{2,1,0:T(8,128)S(1)} %fusion.31, f32[2,576,576]{2,1,0:T(8,128)S(1)} %copy-done, f32[2]{0:T(128)S(1)} %get-tuple-element.10, f32[576,576]{1,0:T(8,128)S(1)} %broadcast_select_fusion), kind=kOutput, calls=%fused_computation.30 | convolution fusion | flops 4589789184 | bytes 11943944 | tf_op jit(solution)/shard_map/dot_general | solution.py:78
  227.3 8.7 %fusion.114 = f32[2,576,576]{2,1,0:T(8,128)S(1)} fusion(f32[2,576,576]{2,1,0:T(8,128)S(1)} %fusion.24), kind=kOutput, calls=%fused_computation.147 | convolution fusion | flops 4586471424 | bytes 5308416 | tf_op jit(solution)/shard_map/dot_general | solution.py:32
  236.0 8.7 %fusion.19 = f32[2,576,576]{2,1,0:T(8,128)S(1)} fusion(f32[2,576,576]{2,1,0:T(8,128)S(1)} %fusion.24, f32[2,576,576]{2,1,0:T(8,128)S(1)} %fusion.114, f32[576,576]{1,0:T(8,128)S(1)} %broadcast_select_fusion), kind=kOutput, calls=%fused_computation.24 | convolution fusion | flops 4589125632 | bytes 9289728 | tf_op jit(solution)/shard_map/dot_general | solution.py:77
  244.7 4.5 fusion.77
  249.2 4.0 fusion.78
  253.2 8.7 %fusion.18 = f32[2,576,576]{2,1,0:T(8,128)S(1)} fusion(f32[2,576,576]{2,1,0:T(8,128)S(1)} %fusion.19, f32[2,576,576]{2,1,0:T(8,128)S(1)} %fusion.114, f32[2,576,576]{2,1,0:T(8,128)S(1)} %fusion.24, f32[576,576]{1,0:T(8,128)S(1)} %broadcast_select_fusion), kind=kOutput, calls=%fused_computation.23 | convolution fusion | flops 4589125632 | bytes 11943936 | tf_op jit(solution)/shard_map/dot_general | solution.py:78
  261.9 8.6 %fusion.115 = f32[2,576,576]{2,1,0:T(8,128)S(1)} fusion(f32[2,576,576]{2,1,0:T(8,128)S(1)} %fusion.18), kind=kOutput, calls=%fused_computation.148 | convolution fusion | flops 4586471424 | bytes 5308416 | tf_op jit(solution)/shard_map/dot_general | solution.py:32
  270.6 8.9 %fusion.13 = f32[2,576,576]{2,1,0:T(8,128)S(1)} fusion(f32[2,576,576]{2,1,0:T(8,128)S(1)} %fusion.18, f32[2,576,576]{2,1,0:T(8,128)S(1)} %fusion.115, f32[576,576]{1,0:T(8,128)S(1)} %broadcast_select_fusion), kind=kOutput, calls=%fused_computation.17 | convolution fusion | flops 4589125632 | bytes 9289728 | tf_op jit(solution)/shard_map/dot_general | solution.py:77
  279.5 4.0 fusion.79
  283.5 9.1 %fusion.12 = f32[2,576,576]{2,1,0:T(8,128)S(1)} fusion(f32[2,576,576]{2,1,0:T(8,128)S(1)} %fusion.13, f32[2,576,576]{2,1,0:T(8,128)S(1)} %fusion.115, f32[2,576,576]{2,1,0:T(8,128)S(1)} %fusion.18, f32[576,576]{1,0:T(8,128)S(1)} %broadcast_select_fusion), kind=kOutput, calls=%fused_computation.16 | convolution fusion | flops 4589125632 | bytes 11943936 | tf_op jit(solution)/shard_map/dot_general | solution.py:78
  292.7 8.5 %fusion.116 = f32[2,576,576]{2,1,0:T(8,128)S(1)} fusion(f32[2,576,576]{2,1,0:T(8,128)S(1)} %fusion.12), kind=kOutput, calls=%fused_computation.149 | convolution fusion | flops 4586471424 | bytes 5308416 | tf_op jit(solution)/shard_map/dot_general | solution.py:32
  301.1 8.9 %fusion.7 = f32[2,576,576]{2,1,0:T(8,128)S(1)} fusion(f32[2,576,576]{2,1,0:T(8,128)S(1)} %fusion.12, f32[2,576,576]{2,1,0:T(8,128)S(1)} %fusion.116, f32[576,576]{1,0:T(8,128)S(1)} %broadcast_select_fusion), kind=kOutput, calls=%fused_computation.10 | convolution fusion | flops 4589125632 | bytes 9289728 | tf_op jit(solution)/shard_map/dot_general | solution.py:77
  310.1 4.0 fusion.80
  314.1 9.0 %fusion.6 = f32[2,576,576]{2,1,0:T(8,128)S(1)} fusion(f32[2,576,576]{2,1,0:T(8,128)S(1)} %fusion.7, f32[2,576,576]{2,1,0:T(8,128)S(1)} %fusion.116, f32[2,576,576]{2,1,0:T(8,128)S(1)} %fusion.12, f32[576,576]{1,0:T(8,128)S(1)} %broadcast_select_fusion), kind=kOutput, calls=%fused_computation.9 | convolution fusion | flops 4589125632 | bytes 11943936 | tf_op jit(solution)/shard_map/dot_general | solution.py:78
  323.1 8.7 %fusion.117 = f32[2,576,576]{2,1,0:T(8,128)S(1)} fusion(f32[2,576,576]{2,1,0:T(8,128)S(1)} %fusion.6), kind=kOutput, calls=%fused_computation.150 | convolution fusion | flops 4586471424 | bytes 5308416 | tf_op jit(solution)/shard_map/dot_general | solution.py:32
  331.8 4.0 fusion
  335.9 0.8 copy.52
  336.7 1.9 reshape.128
  338.6 6.6 %all-to-all-start.1 = ((bf16[128,2,756]{2,1,0:T(2,128)(2,1)}), bf16[128,2,756]{2,1,0:T(2,128)(2,1)S(1)}, u32[]{:S(2)}, u32[]{:S(2)}) async-start(bf16[128,2,756]{2,1,0:T(2,128)(2,1)} %reshape.128), calls=%async_computation.1 | async-start | bytes 786432 | tf_op jit(solution)/shard_map/all_to_all | solution.py:82
  345.3 12.2 %all-to-all-done.1 = bf16[128,2,756]{2,1,0:T(2,128)(2,1)S(1)} async-done(((bf16[128,2,756]{2,1,0:T(2,128)(2,1)}), bf16[128,2,756]{2,1,0:T(2,128)(2,1)S(1)}, u32[]{:S(2)}, u32[]{:S(2)}) %all-to-all-start.1) | async-done | bytes 387104 | tf_op jit(solution)/shard_map/all_to_all | solution.py:82
  357.5 0.8 reshape.129
  358.3 0.4 bitcast_bitcast_fusion
  358.7 0.3 copy.58
  359.0 0.7 gather_fusion.1
  359.7 0.2 select_bitcast_fusion
  360.0 1.2 reshape.111
  361.2 96.8 %all-gather.3.cloned.1.call-done = bf16[128,9,7168]{2,1,0:T(8,128)(2,1)} async-done(((bf16[1,9,7168]{2,1,0:T(8,128)(2,1)}), bf16[128,9,7168]{2,1,0:T(8,128)(2,1)}) %all-gather.3.cloned.1.call-update) | async-done | bytes 16515088 | tf_op jit(solution)/shard_map/all_gather | solution.py:85
  458.0 22.9 %reshape.112 = bf16[1152,7168]{1,0:T(8,128)(2,1)} reshape(bf16[128,9,7168]{2,1,0:T(8,128)(2,1)} %all-gather.3.cloned.1.call-done) | data formatting | bytes 33030144
  (24 shorter events, 1.3 us)
Async XLA Ops:
  15.9 23.8 %all-to-all-start = ((bf16[128,2,756]{2,1,0:T(2,128)(2,1)}), bf16[128,2,756]{2,1,0:T(2,128)(2,1)S(1)}, u32[]{:S(2)}, u32[]{:S(2)}) async-start(bf16[128,2,756]{2,1,0:T(2,128)(2,1)} %reshape.126), calls=%async_computation | async-start | bytes 786432 | tf_op jit(solution)/shard_map/all_to_all | solution.py:60
  27.4 169.8 %all-reduce.2.cloned.1.call-start = ((), (), s32[]{:S(2)}) async-start(), calls=%async_computation.2 | async-start | bytes 5898240 | tf_op jit(solution)/shard_map/psum | solution.py:28
  43.6 5.3 %copy-start.1 = (f32[3,56,1152]{2,1,0:T(8,128)}, f32[3,56,1152]{2,1,0:T(8,128)S(1)}, u32[]{:S(2)}) copy-start(f32[3,56,1152]{2,1,0:T(8,128)S(1)} %add_multiply_fusion) | copy-start | bytes 2322436
  197.3 2.7 copy-start
  338.6 18.9 %all-to-all-start.1 = ((bf16[128,2,756]{2,1,0:T(2,128)(2,1)}), bf16[128,2,756]{2,1,0:T(2,128)(2,1)S(1)}, u32[]{:S(2)}, u32[]{:S(2)}) async-start(bf16[128,2,756]{2,1,0:T(2,128)(2,1)} %reshape.128), calls=%async_computation.1 | async-start | bytes 786432 | tf_op jit(solution)/shard_map/all_to_all | solution.py:82
  345.2 112.8 %all-gather.3.cloned.1.call-start = ((), (), s32[]{:S(2)}) async-start(), calls=%async_computation.3 | async-start | bytes 29589504 | tf_op jit(solution)/shard_map/all_gather | solution.py:85
Sparse Core Ops, SparseCore 0:
  49.0 148.2 all-reduce.1
  361.3 96.6 all-gather.2

commit v2 on v0

v2 whole, which is shorter than its diff:
```python
import math

import jax
import jax.numpy as jnp
from jax import lax
from jax.experimental import pallas as pl
from jax.experimental.pallas import tpu as pltpu
from jax.sharding import PartitionSpec as P

R = 576
ITERS = 5
RP = 640
DEVICES = 128
CHIPS = 64
CORES_TILES = 35
MESH = pl.DeviceIdType.MESH
F32 = jnp.float32
BF16 = jnp.bfloat16

coef_a = 3.4445
coef_b = -4.775
coef_c = 2.0315
epsilon = 1e-07


def position():
    me = lax.axis_index("dp")
    return me, me // 2, lax.rem(me, 2)


def remote(src, dst, send, recv, to):
    return pltpu.make_async_remote_copy(
        src, dst, send, recv, device_id=(to,), device_id_type=MESH
    )


def drain(view, sem):
    pltpu.make_async_copy(view, view, sem).wait()


def greet_all(me):
    barrier = pltpu.get_barrier_semaphore()

    def greet(i, carry):
        pl.semaphore_signal(
            barrier, inc=1, device_id=(jnp.bitwise_xor(me, i),), device_id_type=MESH
        )
        return carry

    lax.fori_loop(1, DEVICES, greet, 0)
    pl.semaphore_wait(barrier, DEVICES - 1)


def split(value):
    high = value.astype(BF16)
    return high, (value - high.astype(F32)).astype(BF16)


def dot(a, b):
    return jnp.dot(a, b, preferred_element_type=F32)


def window_start(t):
    return min(128 * t // 9, DEVICES - 16)


def scatter_kernel(out_ref, mom_ref, mine_ref, fresh_ref, got, place, send, recv):
    me, _, _ = position()
    greet_all(me)

    def push(i, carry):
        to = jnp.bitwise_xor(me, i)
        remote(out_ref.at[to], got.at[me], send, recv, to).start()
        return carry

    lax.fori_loop(1, DEVICES, push, 0)
    got[pl.ds(me, 1)] = out_ref[pl.ds(me, 1)]
    rows = lax.broadcasted_iota(jnp.int32, (256, 128), 0)
    lanes = lax.broadcasted_iota(jnp.int32, (1, 128), 1)
    for t in range(9):
        line = lanes + 128 * t
        source = lax.shift_right_logical(line * 7282, 16)
        r = line - 9 * source
        half = lax.shift_right_logical(r, 1)
        odd = r - 2 * half
        base = 16 * (source - window_start(t)) + half
        for k in range(3):
            for parity in range(2):
                target = jnp.where(odd == parity, base + 5 * k, -1)
                place[t, :, pl.ds(128 * (2 * k + parity), 128)] = jnp.where(
                    rows == target, 1.0, 0.0
                ).astype(BF16)
    others = got.at[pl.ds(0, DEVICES - 1)]
    drain(others, recv)
    for t in range(9):
        window = got[pl.ds(window_start(t), 16)].reshape(256, 128)
        placed = lax.dot_general(
            window, place[t], (((0,), (0,)), ((), ())), preferred_element_type=F32
        )
        for k in range(3):
            arrived = (
                placed[0:56, 256 * k : 256 * k + 128]
                + placed[64:120, 256 * k + 128 : 256 * k + 256]
            )
            fresh_ref[k, :, pl.ds(128 * t, 128)] = (
                0.95 * mom_ref[k, :, pl.ds(128 * t, 128)] + arrived
            ) * mine_ref[k]
    drain(others, send)


def scatter(outgoing, momentum, mine):
    return pl.pallas_call(
        scatter_kernel,
        out_shape=jax.ShapeDtypeStruct(momentum.shape, F32),
        in_specs=[
            pl.BlockSpec(memory_space=pltpu.VMEM),
            pl.BlockSpec(memory_space=pltpu.VMEM),
            pl.BlockSpec(memory_space=pltpu.SMEM),
        ],
        out_specs=pl.BlockSpec(memory_space=pltpu.VMEM),
        scratch_shapes=[
            pltpu.VMEM((DEVICES, 16, 128), BF16),
            pltpu.VMEM((9, 256, 768), BF16),
            pltpu.SemaphoreType.DMA,
            pltpu.SemaphoreType.DMA,
        ],
        compiler_params=pltpu.CompilerParams(
            collective_id=0, has_side_effects=True, vmem_limit_bytes=40 * 2**20
        ),
        name="scatter",
    )(outgoing, momentum, mine)


def align_layer(value, core):
    moved = pltpu.roll(value, (RP - 64) * core, 1)
    lane = lax.broadcasted_iota(jnp.int32, value.shape, 1)
    return jnp.where(lane < R, moved, 0.0)


STRIP = (0, 576, 1024, 1344)


def pack(gram, packed):
    lane = lax.broadcasted_iota(jnp.int32, (64, 128), 1)
    corner = pltpu.roll(gram[512:576, 512:640], 64, 1)
    packed[0:64, :] = jnp.where(lane < 64, gram[0:64, 0:128], corner)
    packed[64:576, :] = gram[64:576, 0:128]
    for s in range(1, 4):
        packed[STRIP[s] : STRIP[s] + 576 - 128 * s, :] = gram[
            128 * s : 576, 128 * s : 128 * s + 128
        ]


def unpack(packed, gram):
    row = lax.broadcasted_iota(jnp.int32, (128, 128), 0)
    lane = lax.broadcasted_iota(jnp.int32, (128, 128), 1)
    upper = (row < 64) & (lane >= 64)
    first = packed[0:128, :]
    clean = jnp.where(upper, 0.0, first)
    gram[0:128, 0:128] = jnp.where(upper, clean.T, clean)
    corner = pltpu.roll(packed[0:64, :], 64, 1)
    lane64 = lax.broadcasted_iota(jnp.int32, (64, 128), 1)
    gram[512:576, 512:640] = jnp.where(lane64 < 64, corner, 0.0)
    gram[576:640, :] = jnp.zeros((64, RP), F32)
    for s in range(4):
        for b in range(s, 5):
            if b == s:
                if s:
                    gram[128 * s : 128 * s + 128, 128 * s : 128 * s + 128] = packed[
                        STRIP[s] : STRIP[s] + 128, :
                    ]
                continue
            n = 64 if b == 4 else 128
            start = STRIP[s] + 128 * (b - s)
            block = packed[start : start + n, :]
            gram[128 * b : 128 * b + n, 128 * s : 128 * s + 128] = block
            if n == 64:
                block = jnp.concatenate([block, jnp.zeros((64, 128), F32)], axis=0)
            gram[128 * s : 128 * s + 128, 128 * b : 128 * b + 128] = block.T


def left_form(value, ref):
    high, low = split(value)
    ref[:, 0:RP] = high
    ref[:, RP : 2 * RP] = high
    ref[:, 2 * RP : 3 * RP] = low


def right_form(value, ref):
    high, low = split(value)
    ref[0:RP, :] = high
    ref[RP : 2 * RP, :] = low
    ref[2 * RP : 3 * RP, :] = high


def iterate_kernel(
    fresh_ref, slot_ref, tile_ref,
    columns, packed, terms, summed, relay, chosen, mcol, gram, ga, gb, pb, ta, xa,
    swap_send, swap_recv, rs_send, rs_recv, ag_send, ag_recv, h1_send, h1_recv, h2_send, h2_recv,
):
    me, chip, core = position()
    greet_all(me)
    sibling = chip * 2 + 1 - core
    mine_lanes = pl.ds(pl.multiple_of(512 * core, 128), RP)
    their_lanes = pl.ds(pl.multiple_of(512 * (1 - core), 128), RP)
    swap = remote(fresh_ref.at[:, :, their_lanes], columns.at[1], swap_send, swap_recv, sibling)
    swap.start()

    def to_relay(i, carry):
        layer = i // CORES_TILES
        u = lax.rem(i, CORES_TILES)
        t = u // 7 + 4 * layer
        q = lax.rem(u, 7)
        to = jnp.where(layer == 0, u * 2 + 1, (63 - u) * 2)
        src = fresh_ref.at[:, pl.ds(pl.multiple_of(8 * q, 8), 8), pl.ds(pl.multiple_of(128 * t, 128), 128)]
        dst = relay.at[pl.ds(3 * me, 3)]

        @pl.when(to != me)
        def _():
            remote(src, dst, h1_send, h1_recv, to).start()

        @pl.when(to == me)
        def _():
            pltpu.make_async_copy(src, dst, h1_recv).start()

        return carry

    lax.fori_loop(0, 2 * CORES_TILES, to_relay, 0)

    columns[0] = fresh_ref[:, :, mine_lanes]
    swap.wait_recv()
    both = align_layer(columns[...].reshape(336, RP), core)
    high, low = split(both)
    gram[...] = lax.dot_general(
        jnp.concatenate([high, high, low], axis=0),
        jnp.concatenate([high, low, high], axis=0),
        (((0,), (0,)), ((), ())),
        preferred_element_type=F32,
    )
    pack(gram, packed)

    def share(c):
        return pl.ds(pl.multiple_of(24 * c, 8), 24)

    def reduce_push(i, carry):
        to = jnp.bitwise_xor(chip, i)
        remote(packed.at[share(to)], terms.at[chip], rs_send, rs_recv, to * 2 + core).start()
        return carry

    lax.fori_loop(1, CHIPS, reduce_push, 0)
    terms[pl.ds(chip, 1)] = packed[share(chip)][None]
    drain(terms.at[pl.ds(0, CHIPS - 1)], rs_recv)
    summed[share(chip)] = jnp.sum(terms[...], axis=0)

    def gather_push(i, carry):
        to = jnp.bitwise_xor(chip, i)
        part = summed.at[share(chip)]
        remote(part, part, ag_send, ag_recv, to * 2 + core).start()
        return carry

    lax.fori_loop(1, CHIPS, gather_push, 0)

    layer = 1 - core
    u = jnp.where(layer == 0, chip, 63 - chip)
    lane_tile = u // 7
    q = lax.rem(u, 7)

    @pl.when(u < CORES_TILES)
    def _():
        drain(relay, h1_recv)

        def choose(b, carry):
            chosen[pl.ds(b, 1)] = relay[pl.ds(slot_ref[b], 1)]
            return carry

        lax.fori_loop(0, DEVICES, choose, 0)

        def to_columns(b, carry):
            octet = 7 * b + q
            to = (octet // 16) * 2 + layer
            dst = mcol.at[
                pl.ds(pl.multiple_of(8 * lax.rem(octet, 16), 8), 8),
                pl.ds(pl.multiple_of(128 * lane_tile, 128), 128),
            ]
            remote(chosen.at[b], dst, h2_send, h2_recv, to).start()
            return carry

        lax.fori_loop(0, DEVICES, to_columns, 0)

    drain(summed.at[pl.ds(0, 24 * (CHIPS - 1))], ag_recv)
    unpack(summed, gram)

    diag = lax.broadcasted_iota(jnp.int32, (RP, RP), 0) == lax.broadcasted_iota(jnp.int32, (RP, RP), 1)
    squares = jnp.sum(jnp.where(diag, gram[...], 0.0), axis=(0, 1), keepdims=True)
    inverse = 1.0 / (jnp.sqrt(squares) + epsilon)
    gram[...] = gram[...] * (inverse * inverse)

    @pl.when(chip < 56)
    def _():
        drain(mcol, h2_recv)

    @pl.when(chip >= 56)
    def _():
        mcol[...] = jnp.zeros_like(mcol)

    left_form(align_layer(mcol[...], core) * inverse, xa)

    def polynomial():
        g = gram[...]
        left_form(g, ga)
        right_form(g, gb)
        p = coef_b * g + coef_c * dot(ga[...], gb[...])
        right_form(jnp.where(diag, p + coef_a, p), pb)

    def sweep(i, carry):
        polynomial()
        left_form(dot(xa[...], pb[...]), xa)
        left_form(dot(ga[...], pb[...]), ta)
        gram[...] = dot(ta[...], pb[...])
        return carry

    lax.fori_loop(0, ITERS - 1, sweep, 0)
    polynomial()
    result = dot(xa[...], pb[...]) * (0.2 * math.sqrt(max(R, 7168)))
    tile_ref[...] = result.T[0:R, :].astype(BF16)

    swap.wait_send()
    drain(terms.at[pl.ds(0, CHIPS - 1)], rs_send)
    drain(summed.at[pl.ds(0, 24 * (CHIPS - 1))], ag_send)

    @pl.when(u < CORES_TILES)
    def _():
        drain(relay.at[pl.ds(0, 3 * (2 * CORES_TILES - 1))], h1_send)
        drain(chosen, h2_send)

    @pl.when(u >= CORES_TILES)
    def _():
        drain(relay.at[pl.ds(0, 3 * 2 * CORES_TILES)], h1_send)


def iterate(fresh, slot_index):
    return pl.pallas_call(
        iterate_kernel,
        out_shape=jax.ShapeDtypeStruct((R, 128), BF16),
        in_specs=[
            pl.BlockSpec(memory_space=pltpu.VMEM),
            pl.BlockSpec(memory_space=pltpu.SMEM),
        ],
        out_specs=pl.BlockSpec(memory_space=pltpu.VMEM),
        scratch_shapes=[
            pltpu.VMEM((2, 3, 56, RP), F32),
            pltpu.VMEM((1536, 128), F32),
            pltpu.VMEM((CHIPS, 24, 128), F32),
            pltpu.VMEM((1536, 128), F32),
            pltpu.VMEM((384, 8, 128), F32),
            pltpu.VMEM((DEVICES, 8, 128), F32),
            pltpu.VMEM((128, RP), F32),
            pltpu.VMEM((RP, RP), F32),
            pltpu.VMEM((RP, 3 * RP), BF16),
            pltpu.VMEM((3 * RP, RP), BF16),
            pltpu.VMEM((3 * RP, RP), BF16),
            pltpu.VMEM((RP, 3 * RP), BF16),
            pltpu.VMEM((128, 3 * RP), BF16),
        ]
        + [pltpu.SemaphoreType.DMA] * 10,
        compiler_params=pltpu.CompilerParams(
            collective_id=1, has_side_effects=True, vmem_limit_bytes=50 * 2**20
        ),
        name="iterate",
    )(fresh, slot_index)


ORDERS = ("xyz", "yzx", "zxy")


def gather_kernel(tile_ref, out, local_sem, send, recv, sib_send, sib_recv):
    me, chip, core = position()
    home = {"y": chip // 16, "z": lax.rem(chip // 4, 4), "x": lax.rem(chip, 4)}
    sibling = chip * 2 + 1 - core

    def shift(axis, step):
        moved = dict(home)
        moved[axis] = lax.rem(home[axis] + step + 4, 4)
        return moved

    def device(at):
        return ((at["y"] * 4 + at["z"]) * 4 + at["x"]) * 2 + core

    barrier = pltpu.get_barrier_semaphore()
    for other in [device(shift(axis, step)) for axis in "yzx" for step in (1, -1)] + [sibling]:
        pl.semaphore_signal(barrier, inc=1, device_id=(other,), device_id_type=MESH)
    pl.semaphore_wait(barrier, 7)

    def held(part, phase, at):
        y, z, x = at["y"], at["z"], at["x"]
        if phase == 0:
            return [(128 * (16 * y + 4 * z + x), 128)]
        if part == 0:
            if phase == 1:
                return [(512 * (4 * y + z), 512)]
            return [(512 * (4 * s + z), 512) for s in range(4)]
        if part == 1:
            if phase == 1:
                return [(128 * (16 * s + 4 * z + x), 128) for s in range(4)]
            return [(128 * (16 * s + 4 * t + x), 128) for s in range(4) for t in range(4)]
        if phase == 1:
            return [(128 * (16 * y + 4 * s + x), 128) for s in range(4)]
        return [(2048 * y, 2048)]

    def view(part, columns, half):
        row = R * core + 192 * part + (0 if half is None else 96 * half)
        return out.at[
            pl.ds(pl.multiple_of(row, 16), 192 if half is None else 96),
            pl.ds(pl.multiple_of(columns[0], 128), columns[1]),
        ]

    def push(part, columns, send_sem, recv_sem, to, half=None):
        for item in columns:
            block = view(part, item, half)
            remote(block, block, send_sem, recv_sem, to).start()

    def drain_size(sem, rows, width):
        drain(out.at[pl.ds(0, rows), pl.ds(0, width)], sem)

    own = pltpu.make_async_copy(
        tile_ref,
        out.at[pl.ds(pl.multiple_of(R * core, 16), R), pl.ds(pl.multiple_of(128 * chip, 128), 128)],
        local_sem,
    )
    own.start()
    own.wait()
    sides = ((0, 1), (1, -1))
    for phase in range(3):
        width = 128 * 4**phase
        for part in range(3):
            axis = ORDERS[part][phase]
            for d, step in sides:
                push(part, held(part, phase, home), send.at[part, phase, 0, d], recv.at[part, phase, 0, d], device(shift(axis, step)))
        if phase == 2:
            for part in range(3):
                push(part, held(part, 2, home), sib_send.at[part], sib_recv.at[part], sibling)
        for part in range(3):
            axis = ORDERS[part][phase]
            for d, step in sides:
                drain_size(recv.at[part, phase, 0, d], 192, width)
                arrived = held(part, phase, shift(axis, -step))
                push(part, arrived, send.at[part, phase, 1, d], recv.at[part, phase, 1, d], device(shift(axis, step)), half=d)
                if phase == 2:
                    n = 3 + 2 * part + d
                    push(part, arrived, sib_send.at[n], sib_recv.at[n], sibling)
        for part in range(3):
            axis = ORDERS[part][phase]
            for d, step in sides:
                drain_size(recv.at[part, phase, 1, d], 96, width)
                if phase == 2:
                    n = 9 + 2 * part + d
                    push(part, held(part, phase, shift(axis, -2 * step)), sib_send.at[n], sib_recv.at[n], sibling, half=d)
    for part in range(3):
        for phase in range(3):
            for d in range(2):
                drain_size(send.at[part, phase, 0, d], 192, 128 * 4**phase)
                drain_size(send.at[part, phase, 1, d], 96, 128 * 4**phase)
    for n in range(15):
        drain_size(sib_send.at[n], 192 if n < 9 else 96, 2048)
        drain_size(sib_recv.at[n], 192 if n < 9 else 96, 2048)


def gather(tile):
    return pl.pallas_call(
        gather_kernel,
        out_shape=jax.ShapeDtypeStruct((2 * R, 128 * CHIPS), BF16),
        in_specs=[pl.BlockSpec(memory_space=pltpu.VMEM)],
        out_specs=pl.BlockSpec(memory_space=pl.ANY),
        scratch_shapes=[
            pltpu.SemaphoreType.DMA,
            pltpu.SemaphoreType.DMA((3, 3, 2, 2)),
            pltpu.SemaphoreType.DMA((3, 3, 2, 2)),
            pltpu.SemaphoreType.DMA((15,)),
            pltpu.SemaphoreType.DMA((15,)),
        ],
        compiler_params=pltpu.CompilerParams(
            collective_id=2, has_side_effects=True, vmem_limit_bytes=50 * 2**20
        ),
        name="gather",
    )(tile)


def slot_of_blocks(table, slot_count):
    positions = jnp.arange(table.shape[0], dtype=jnp.int32)
    matching = (table[None, :] == table[:, None]) & (positions[None, :] < positions[:, None])
    ranking = jnp.sum(matching.astype(jnp.int32), axis=1)
    return table * slot_count + ranking


def local(grads, momentum, table):
    me = lax.axis_index("dp")
    slot_index = slot_of_blocks(table, 3)
    hits = slot_index[None, :] == jnp.arange(384, dtype=jnp.int32)[:, None]
    count = jnp.sum((table == me).astype(jnp.int32))
    mine = (jnp.arange(3, dtype=jnp.int32) < count).astype(F32)
    pieces = jnp.pad(grads.reshape(9, 128, 56), ((0, 1), (0, 0), (0, 8)))
    pieces = pieces.transpose(1, 0, 2).reshape(128, 640)
    outgoing = jnp.dot(hits.astype(BF16), pieces, preferred_element_type=F32).astype(BF16)
    outgoing = jnp.pad(outgoing.reshape(128, 15, 128), ((0, 0), (0, 1), (0, 0)))
    fresh = scatter(outgoing, momentum, mine)
    tile = iterate(fresh, slot_index)
    update = gather(tile)[:, :7168]
    return update, fresh


def solution(mesh):
    in_specs = (P("dp", None), P("dp", None, None), P())
    out_specs = (P(), P("dp", None, None))
    return jax.shard_map(local, mesh=mesh, in_specs=in_specs, out_specs=out_specs, check_vma=False)
```

time: 1120 us -> 186 us (0.17)
  waiting for transfers between devices: 870 us -> 0 us
  Pallas kernels: 0 us -> 164 us
  matrix products: 98 us -> 0.31 us
  blocking collectives: 62.9 us -> 0 us
  local copies, waits for them, and re-layouts: 38.2 us -> 17.9 us
  starting transfers between devices: 19.3 us -> 0 us
  between operations: 14.9 us -> 0.73 us
    psum x5 -> x0, waiting for transfers between devices: 749 us -> none  [gram_sum(): return lax.psum(partial_gram, 'dp')]
    pallas_call x0 -> x3, Pallas kernels: none -> 164 us  [the longest x1 85.8 us: iterate(): pl.pallas_call(iterate_kernel, out_shape=jax.ShapeDtypeStruct((R, 128), B...]
    all_gather x1 -> x0, waiting for transfers between devices: 96.8 us -> none  [local(): update = lax.all_gather(ordered, 'dp', axis=0, tiled=True)]
    dot_general x10 -> x1, matrix products: 78.9 us -> 0.31 us  [local(): jnp.dot(hits.astype(BF16), pieces, preferred_element_type=F32).astype(BF16)]
    psum x1 -> x0, blocking collectives: 62.9 us -> none  [local(): squares = lax.psum(jnp.sum(per_layer * per_layer, axis=(0, 1, 3)), 'dp')]
    unnamed x18 -> x3, local copies, waits for them, and re-layouts: 29.3 us -> 2 us
    all_to_all x2 -> x0, waiting for transfers between devices: 24.4 us -> none  [the longest x1 12.2 us: local(): lax.all_to_all(going_back, 'dp', split_axis=2, concat_axis=0, tiled=True)]
    unnamed x5 -> x0, matrix products: 19.1 us -> none
  transfers between devices with their start and end apart: 8 -> 0, of which waited for: 8 -> 0; matrix products, arithmetic and copies ran while one was open for 0% -> 0% of each run, Pallas kernels for 0% -> 0%
where the time goes in v2:
time: 186 us
  Pallas kernels  164 us (88%)
  local copies, waits for them, and re-layouts  17.9 us (10%)
  other arithmetic  2.85 us (2%)
    pallas_call x1, Pallas kernels, iterate(): pl.pallas_call(iterate_kernel, out_shape=jax.ShapeDtypeStruct((R, 128), B...  85.8 us
    pallas_call x1, Pallas kernels, gather(): pl.pallas_call(gather_kernel, out_shape=jax.ShapeDtypeStruct((2 * R, 128...  55.7 us
    pallas_call x1, Pallas kernels, scatter(): pl.pallas_call(scatter_kernel, out_shape=jax.ShapeDtypeStruct(momentum.sh...  22.4 us
    slice x1, local copies, waits for them, and re-layouts, local(): update = gather(tile)[:, :7168]  13.6 us

profile of v2, /device:TPU:1, one launch (start us, length us, event | category | flops | bytes accessed | tf_op | source)
XLA Modules:
  0.0 185.6 jit_solution(9685025814108484520)
XLA Ops:
  0.6 0.9 convert_reduce_fusion
  1.5 1.3 fusion.2
  2.8 0.6 compare_convert_fusion.mine_ref
  3.5 1.5 reshape.16
  5.0 0.1 pad_bitcast_fusion
  5.1 0.2 copy.6
  5.2 0.3 convolution_convert_fusion
  5.6 0.4 reshape.18
  6.0 0.1 pad.9.out_ref
  6.1 0.0 copy-start
  6.1 1.1 copy-done
  7.2 22.4 %scatter.1.fresh_ref = f32[3,56,1152]{2,1,0:T(8,128)S(1)} custom-call(bf16[128,16,128]{2,1,0:T(8,128)(2,1)S(1)} %pad.9.out_ref, f32[3,56,1152]{2,1,0:T(8,128)S(1)} %copy-done, f32[3]{0:T(128)S(1)} %compare_convert_fusion.mine_ref), custom_call_target="tpu_custom_call" | custom-call | tf_op jit(solution)/shard_map/scatter/pallas_call | solution.py:112
  29.6 85.8 %iterate.1.tile_ref = bf16[576,128]{1,0:T(8,128)(2,1)S(1)} custom-call(f32[3,56,1152]{2,1,0:T(8,128)S(1)} %scatter.1.fresh_ref, s32[128]{0:T(128)S(1)} %get-tuple-element.3.slot_ref), custom_call_target="tpu_custom_call" | custom-call | tf_op jit(solution)/shard_map/iterate/pallas_call | solution.py:342
  115.4 55.7 %gather.1 = bf16[1152,8192]{1,0:T(8,128)(2,1)} custom-call(bf16[576,128]{1,0:T(8,128)(2,1)S(1)} %iterate.1.tile_ref), custom_call_target="tpu_custom_call" | custom-call | tf_op jit(solution)/shard_map/gather/pallas_call | solution.py:469
  171.1 13.6 %slice.3 = bf16[1152,7168]{1,0:T(8,128)(2,1)} slice(bf16[1152,8192]{1,0:T(8,128)(2,1)} %gather.1), slice={[0:1152], [0:7168]} | slice | bytes 33030144 | tf_op jit(solution)/shard_map/slice | solution.py:507
  184.8 0.9 copy.8
Async XLA Ops:
  6.1 1.1 copy-start

commit v3 on v0

v3 whole, which is shorter than its diff:
```python
import math

import jax
import jax.numpy as jnp
from jax import lax
from jax.experimental import pallas as pl
from jax.experimental.pallas import tpu as pltpu
from jax.sharding import PartitionSpec as P

R = 576
ITERS = 5
RP = 640
K3 = 1792
DEVICES = 128
CHIPS = 64
TILES = 56
RELAYS = 35
MESH = pl.DeviceIdType.MESH
F32 = jnp.float32
BF16 = jnp.bfloat16

coef_a = 3.4445
coef_b = -4.775
coef_c = 2.0315
epsilon = 1e-07


def position():
    me = lax.axis_index("dp")
    return me, me // 2, lax.rem(me, 2)


def remote(src, dst, send, recv, to):
    return pltpu.make_async_remote_copy(
        src, dst, send, recv, device_id=(to,), device_id_type=MESH
    )


def drain(view, sem):
    pltpu.make_async_copy(view, view, sem).wait()


def split(value):
    high = value.astype(BF16)
    return high, (value - high.astype(F32)).astype(BF16)


def dot(a, b):
    return jnp.dot(a, b, preferred_element_type=F32)


def window_start(t):
    return min(128 * t // 9, DEVICES - 16)


def align_layer(value, core):
    moved = pltpu.roll(value, (RP - 64) * core, 1)
    lane = lax.broadcasted_iota(jnp.int32, value.shape, 1)
    return jnp.where(lane < R, moved, 0.0)


STRIP = (0, 576, 1024, 1344)


def pack(gram, packed):
    lane = lax.broadcasted_iota(jnp.int32, (64, 128), 1)
    corner = pltpu.roll(gram[512:576, 512:640], 64, 1)
    packed[0:64, :] = jnp.where(lane < 64, gram[0:64, 0:128], corner)
    packed[64:576, :] = gram[64:576, 0:128]
    for s in range(1, 4):
        packed[STRIP[s] : STRIP[s] + 576 - 128 * s, :] = gram[
            128 * s : 576, 128 * s : 128 * s + 128
        ]


def unpack(packed, gram):
    row = lax.broadcasted_iota(jnp.int32, (128, 128), 0)
    lane = lax.broadcasted_iota(jnp.int32, (128, 128), 1)
    upper = (row < 64) & (lane >= 64)
    first = packed[0:128, :]
    clean = jnp.where(upper, 0.0, first)
    gram[0:128, 0:128] = jnp.where(upper, clean.T, clean)
    corner = pltpu.roll(packed[0:64, :], 64, 1)
    lane64 = lax.broadcasted_iota(jnp.int32, (64, 128), 1)
    gram[512:576, 512:640] = jnp.where(lane64 < 64, corner, 0.0)
    for s in range(4):
        for b in range(s, 5):
            if b == s:
                if s:
                    gram[128 * s : 128 * s + 128, 128 * s : 128 * s + 128] = packed[
                        STRIP[s] : STRIP[s] + 128, :
                    ]
                continue
            n = 64 if b == 4 else 128
            start = STRIP[s] + 128 * (b - s)
            block = packed[start : start + n, :]
            gram[128 * b : 128 * b + n, 128 * s : 128 * s + 128] = block
            if n == 64:
                block = jnp.concatenate([block, jnp.zeros((64, 128), F32)], axis=0)
            gram[128 * s : 128 * s + 128, 128 * b : 128 * b + 128] = block.T


def greet_all(me, ready):
    barrier = pltpu.get_barrier_semaphore()
    for i in [*range(1, 16), *range(16, DEVICES, 16)]:
        pl.semaphore_signal(
            barrier, inc=1, device_id=(jnp.bitwise_xor(me, i),), device_id_type=MESH
        )

    def finish():
        pl.semaphore_wait(barrier, 22)
        for i in range(16, DEVICES, 16):
            pl.semaphore_signal(
                ready, inc=1, device_id=(jnp.bitwise_xor(me, i),), device_id_type=MESH
            )
        pl.semaphore_wait(ready, 7)

    return finish


def left_form(value, ref):
    high, low = split(value)
    tail = value[:, 512:RP]
    ref[:, 0:512] = high[:, 0:512]
    ref[:, 512:1024] = high[:, 0:512]
    ref[:, 1024:1536] = low[:, 0:512]
    ref[:, 1536:1664] = (tail + pltpu.roll(tail, 64, 1)).astype(BF16)
    ref[:, 1664:1792] = low[:, 512:RP]


def right_form(value, ref):
    high, low = split(value)
    ref[0:512, :] = high[0:512]
    ref[512:1024, :] = low[0:512]
    ref[1024:1536, :] = high[0:512]
    ref[1536:1600, :] = high[512:R]
    ref[1600:1664, :] = low[512:R]
    ref[1664:1728, :] = high[512:R]


def symmetric_dot(left, right, out):
    c0 = dot(left[...], right[:, 0:256])
    c1 = dot(left[256:R, :], right[:, 256:512])
    c2 = dot(left[512:R, :], right[:, 512:RP])
    blank = jnp.zeros((64, 256), F32)
    out[:, 0:256] = c0
    out[256:R, 256:512] = c1
    out[512:R, 512:RP] = c2
    out[0:256, 256:512] = c0[256:512].T
    out[0:256, 512:RP] = jnp.concatenate([c0[512:R], blank], axis=0).T
    out[256:512, 512:RP] = jnp.concatenate([c1[256:320], blank], axis=0).T


ORDERS = ("xyz", "yzx", "zxy")
OFFSETS = (0, -1, 1, 2)
SIDES = ((0, 1), (1, -1))


def gather_steps(buf, send, recv, sib_send, sib_recv):
    me, chip, core = position()
    home = {"y": chip // 16, "z": lax.rem(chip // 4, 4), "x": lax.rem(chip, 4)}
    sibling = chip * 2 + 1 - core
    parts = range(3)

    def shift(at, axis, step):
        moved = dict(at)
        moved[axis] = lax.rem(at[axis] + step + 4, 4)
        return moved

    def device(at):
        return ((at["y"] * 4 + at["z"]) * 4 + at["x"]) * 2 + core

    def rows_of(part, half):
        row = R * core + 192 * part + (0 if half is None else 96 * half)
        return pl.ds(pl.multiple_of(row, 16), 192 if half is None else 96)

    def line(part, at):
        y, z, x = at["y"], at["z"], at["x"]
        if part == 0:
            return jnp.logical_or(y < 3, z < 2), 4, 0, lambda n: (y, z, pl.ds(0, n))
        if part == 1:
            return z < 2, 4, 3, lambda n: (pl.ds(0, n), z, x)
        return y < 3, 4, 2, lambda n: (y, pl.ds(0, n), x)

    def tile(part, at):
        y, z, x = at["y"], at["z"], at["x"]
        return jnp.logical_or(y < 3, z < 2), 1, 0, lambda n: (y, z, pl.ds(x, n))

    def each(spec, act):
        whole, count, fewer, index = spec

        @pl.when(whole)
        def _():
            act(count, index(count))

        if fewer:

            @pl.when(jnp.logical_not(whole))
            def _():
                act(fewer, index(fewer))

    def push(part, spec, send_sem, recv_sem, to, half=None):
        def act(count, index):
            block = buf.at[(*index, rows_of(part, half))]
            remote(block, block, send_sem, recv_sem, to).start()

        each(spec, act)

    def take(spec, sem, half=None):
        def act(count, index):
            drain(buf.at[0, 0, pl.ds(0, count), pl.ds(0, 192 if half is None else 96)], sem)

        each(spec, act)

    def both(part, k, spec, axis):
        for d, step in SIDES:
            push(part, spec, send.at[part, k, d], recv.at[part, k, d], device(shift(home, axis, step)))

    def pass_on(part, k, spec, d, axis, step):
        push(part, spec, send.at[part, k, d], recv.at[part, k, d], device(shift(home, axis, step)), half=d)

    def tell(part, n, spec, half=None):
        push(part, spec, sib_send.at[part, n], sib_recv.at[part, n], sibling, half=half)

    def near(part, axis, step, i):
        return line(part, shift(shift(home, axis, step), ORDERS[part][1], OFFSETS[i]))

    def forward(part, i):
        axis = ORDERS[part][2]
        for d, step in SIDES:
            got = near(part, axis, -step, i)
            take(got, recv.at[part, 4 + i, d])
            pass_on(part, 8 + i, got, d, axis, step)
            tell(part, 4 + 2 * i + d, got)

    for p in parts:
        both(p, 0, tile(p, home), ORDERS[p][0])
    for p in parts:
        axis = ORDERS[p][0]
        for d, step in SIDES:
            got = tile(p, shift(home, axis, -step))
            take(got, recv.at[p, 0, d])
            pass_on(p, 1, got, d, axis, step)
    for p in parts:
        first, second, third = ORDERS[p]
        for d, step in SIDES:
            take(tile(p, shift(home, first, 2)), recv.at[p, 1, d], half=d)
        both(p, 2, line(p, home), second)
        both(p, 4, line(p, home), third)
        tell(p, 0, line(p, home))
    for p in parts:
        _, second, third = ORDERS[p]
        for d, step in SIDES:
            got = line(p, shift(home, second, -step))
            take(got, recv.at[p, 2, d])
            pass_on(p, 3, got, d, second, step)
            both(p, 5 + d, got, third)
            tell(p, 1 + d, got)
    for p in parts:
        forward(p, 0)
    for p in parts:
        _, second, third = ORDERS[p]
        got = line(p, shift(home, second, 2))
        for d, step in SIDES:
            take(got, recv.at[p, 3, d], half=d)
        both(p, 7, got, third)
        tell(p, 3, got)
    for i in (1, 2, 3):
        for p in parts:
            forward(p, i)
    for i in range(4):
        for p in parts:
            got = near(p, ORDERS[p][2], 2, i)
            for d, step in SIDES:
                take(got, recv.at[p, 8 + i, d], half=d)
                tell(p, 12 + 2 * i + d, got, half=d)

    for p in parts:
        first, second, third = ORDERS[p]
        for d, step in SIDES:
            take(tile(p, home), send.at[p, 0, d])
            take(tile(p, shift(home, first, -step)), send.at[p, 1, d], half=d)
            take(line(p, home), send.at[p, 2, d])
            take(line(p, shift(home, second, -step)), send.at[p, 3, d], half=d)
            for i in range(4):
                take(near(p, third, 0, i), send.at[p, 4 + i, d])
                take(near(p, third, -step, i), send.at[p, 8 + i, d], half=d)
        for sem in (sib_send, sib_recv):
            for i in range(4):
                take(near(p, third, 0, i), sem.at[p, i])
                for d, step in SIDES:
                    take(near(p, third, -step, i), sem.at[p, 4 + 2 * i + d])
                    take(near(p, third, 2, i), sem.at[p, 12 + 2 * i + d], half=d)


def step_kernel(
    out_ref, mom_ref, mine_ref, slot_ref, fresh_ref, buf,
    got, place, columns, packed, terms, summed, relay, chosen, arrived, mcol,
    gram, gram2, ga, gb, pbs, ta, xa, ready,
    a2a_send, a2a_recv, swap_send, swap_recv, rs_send, rs_recv, ag_send, ag_recv,
    h1_send, h1_recv, h2_send, h2_recv, send, recv, sib_send, sib_recv,
):
    me, chip, core = position()
    greeted = greet_all(me, ready)

    rows = lax.broadcasted_iota(jnp.int32, (256, 128), 0)
    lanes = lax.broadcasted_iota(jnp.int32, (1, 128), 1)
    for t in range(9):
        row = lanes + 128 * t
        source = lax.shift_right_logical(row * 7282, 16)
        r = row - 9 * source
        half = lax.shift_right_logical(r, 1)
        odd = r - 2 * half
        base = 16 * (source - window_start(t)) + half
        for k in range(3):
            for parity in range(2):
                target = jnp.where(odd == parity, base + 5 * k, -1)
                place[t, :, pl.ds(128 * (2 * k + parity), 128)] = jnp.where(
                    rows == target, 1.0, 0.0
                ).astype(BF16)
    greeted()

    def push(i, carry):
        to = jnp.bitwise_xor(me, i)
        remote(out_ref.at[to], got.at[me], a2a_send, a2a_recv, to).start()
        return carry

    lax.fori_loop(1, DEVICES, push, 0)
    got[pl.ds(me, 1)] = out_ref[pl.ds(me, 1)]
    for i in range(ITERS):
        pbs[i, 1728:K3, :] = jnp.zeros((K3 - 1728, RP), BF16)
    gb[1728:K3, :] = jnp.zeros((K3 - 1728, RP), BF16)
    chosen[DEVICES : DEVICES + 2] = jnp.zeros((2, 8, 128), F32)
    others = got.at[pl.ds(0, DEVICES - 1)]
    drain(others, a2a_recv)
    for t in range(9):
        window = got[pl.ds(window_start(t), 16)].reshape(256, 128)
        placed = lax.dot_general(
            window, place[t], (((0,), (0,)), ((), ())), preferred_element_type=F32
        )
        for k in range(3):
            grad = (
                placed[0:56, 256 * k : 256 * k + 128]
                + placed[64:120, 256 * k + 128 : 256 * k + 256]
            )
            fresh_ref[k, :, pl.ds(128 * t, 128)] = (
                0.95 * mom_ref[k, :, pl.ds(128 * t, 128)] + grad
            ) * mine_ref[k]

    sibling = chip * 2 + 1 - core
    mine_lanes = pl.ds(pl.multiple_of(512 * core, 128), RP)
    their_lanes = pl.ds(pl.multiple_of(512 * (1 - core), 128), RP)
    swap = remote(fresh_ref.at[:, :, their_lanes], columns.at[1], swap_send, swap_recv, sibling)
    swap.start()
    columns[0] = fresh_ref[:, :, mine_lanes]
    swap.wait_recv()
    both = align_layer(columns[...].reshape(336, RP), core)
    high, low = split(both)
    gram[...] = lax.dot_general(
        jnp.concatenate([high, high, low], axis=0),
        jnp.concatenate([high, low, high], axis=0),
        (((0,), (0,)), ((), ())),
        preferred_element_type=F32,
    )[0:R]
    pack(gram, packed)

    def share(c):
        return pl.ds(pl.multiple_of(24 * c, 8), 24)

    def reduce_push(i, carry):
        to = jnp.bitwise_xor(chip, i)
        remote(packed.at[share(to)], terms.at[chip], rs_send, rs_recv, to * 2 + core).start()
        return carry

    lax.fori_loop(1, CHIPS, reduce_push, 0)
    terms[pl.ds(chip, 1)] = packed[share(chip)][None]
    drain(terms.at[pl.ds(0, CHIPS - 1)], rs_recv)
    summed[share(chip)] = jnp.sum(terms[...], axis=0)

    def gather_push(i, carry):
        to = jnp.bitwise_xor(chip, i)
        part = summed.at[share(chip)]
        remote(part, part, ag_send, ag_recv, to * 2 + core).start()
        return carry

    lax.fori_loop(1, CHIPS, gather_push, 0)

    def to_relay(i, carry):
        layer = i // RELAYS
        u = lax.rem(i, RELAYS)
        t = u // 7 + 4 * layer
        q = lax.rem(u, 7)
        to = jnp.where(layer == 0, u * 2 + 1, (63 - u) * 2)
        src = fresh_ref.at[
            :, pl.ds(pl.multiple_of(8 * q, 8), 8), pl.ds(pl.multiple_of(128 * t, 128), 128)
        ]
        dst = relay.at[pl.ds(3 * me, 3)]

        @pl.when(to != me)
        def _():
            remote(src, dst, h1_send, h1_recv, to).start()

        @pl.when(to == me)
        def _():
            pltpu.make_async_copy(src, dst, h1_recv).start()

        return carry

    lax.fori_loop(0, 2 * RELAYS, to_relay, 0)

    drain(summed.at[pl.ds(0, 24 * (CHIPS - 1))], ag_recv)
    unpack(summed, gram)
    diag = lax.broadcasted_iota(jnp.int32, (R, RP), 0) == lax.broadcasted_iota(jnp.int32, (R, RP), 1)
    squares = jnp.sum(jnp.where(diag, gram[...], 0.0), axis=(0, 1), keepdims=True)
    inverse = 1.0 / (jnp.sqrt(squares) + epsilon)
    gram[...] = gram[...] * (inverse * inverse)

    def polynomial(i):
        g = gram[...]
        left_form(g, ga)
        right_form(g, gb)
        symmetric_dot(ga, gb, gram2)
        p = coef_b * g + coef_c * gram2[...]
        right_form(jnp.where(diag, p + coef_a, p), pbs.at[i])

    def sweep(i, carry):
        polynomial(i)
        symmetric_dot(ga, pbs.at[i], gram2)
        left_form(gram2[...], ta)
        symmetric_dot(ta, pbs.at[i], gram)
        return carry

    lax.fori_loop(0, 2, sweep, 0)

    layer = 1 - core
    u = jnp.where(layer == 0, chip, 63 - chip)
    lane_tile = u // 7
    q = lax.rem(u, 7)

    def first_block(j, q):
        return (16 * j - q + 6) // 7

    @pl.when(u < RELAYS)
    def _():
        drain(relay, h1_recv)

        def choose(b, carry):
            chosen[pl.ds(b, 1)] = relay[pl.ds(slot_ref[b], 1)]
            return carry

        lax.fori_loop(0, DEVICES, choose, 0, unroll=8)

        def to_columns(j, carry):
            src = chosen.at[pl.ds(first_block(j, q), 3)]
            remote(src, arrived.at[lane_tile, q], h2_send, h2_recv, j * 2 + layer).start()
            return carry

        lax.fori_loop(0, TILES, to_columns, 0)

    lax.fori_loop(2, ITERS - 1, sweep, 0)
    polynomial(ITERS - 1)

    @pl.when(chip < TILES)
    def _():
        drain(arrived, h2_recv)
        for i in range(16):
            octet = 16 * chip + i
            block = octet // 7
            r = octet - 7 * block
            for t in range(5):
                mcol[8 * i : 8 * i + 8, 128 * t : 128 * t + 128] = arrived[
                    t, r, block - first_block(chip, r)
                ]

    @pl.when(chip >= TILES)
    def _():
        mcol[...] = jnp.zeros_like(mcol)

    value = align_layer(mcol[...], core) * inverse

    def apply(i, value):
        left_form(value, xa)
        return dot(xa[...], pbs[i])

    value = lax.fori_loop(0, ITERS, apply, value) * (0.2 * math.sqrt(max(R, 7168)))
    buf[chip // 16, lax.rem(chip // 4, 4), lax.rem(chip, 4), pl.ds(pl.multiple_of(R * core, 16), R)] = (
        value.T[0:R, :].astype(BF16)
    )
    gather_steps(buf, send, recv, sib_send, sib_recv)

    drain(others, a2a_send)
    swap.wait_send()
    drain(terms.at[pl.ds(0, CHIPS - 1)], rs_send)
    drain(summed.at[pl.ds(0, 24 * (CHIPS - 1))], ag_send)

    @pl.when(u < RELAYS)
    def _():
        drain(relay.at[pl.ds(0, 3 * (2 * RELAYS - 1))], h1_send)
        drain(relay.at[pl.ds(0, 3 * TILES)], h2_send)

    @pl.when(u >= RELAYS)
    def _():
        drain(relay.at[pl.ds(0, 3 * 2 * RELAYS)], h1_send)


def step(outgoing, momentum, mine, slot_index):
    return pl.pallas_call(
        step_kernel,
        out_shape=(
            jax.ShapeDtypeStruct(momentum.shape, F32),
            pltpu.VMEM((4, 4, 4, 2 * R, 128), BF16),
        ),
        in_specs=[
            pl.BlockSpec(memory_space=pltpu.VMEM),
            pl.BlockSpec(memory_space=pltpu.VMEM),
            pl.BlockSpec(memory_space=pltpu.SMEM),
            pl.BlockSpec(memory_space=pltpu.SMEM),
        ],
        out_specs=(
            pl.BlockSpec(memory_space=pltpu.VMEM),
            pl.BlockSpec(memory_space=pltpu.VMEM),
        ),
        scratch_shapes=[
            pltpu.VMEM((DEVICES, 16, 128), BF16),
            pltpu.VMEM((9, 256, 768), BF16),
            pltpu.VMEM((2, 3, 56, RP), F32),
            pltpu.VMEM((1536, 128), F32),
            pltpu.VMEM((CHIPS, 24, 128), F32),
            pltpu.VMEM((1536, 128), F32),
            pltpu.VMEM((384, 8, 128), F32),
            pltpu.VMEM((DEVICES + 2, 8, 128), F32),
            pltpu.VMEM((5, 7, 3, 8, 128), F32),
            pltpu.VMEM((128, RP), F32),
            pltpu.VMEM((R, RP), F32),
            pltpu.VMEM((R, RP), F32),
            pltpu.VMEM((R, K3), BF16),
            pltpu.VMEM((K3, RP), BF16),
            pltpu.VMEM((ITERS, K3, RP), BF16),
            pltpu.VMEM((R, K3), BF16),
            pltpu.VMEM((128, K3), BF16),
            pltpu.SemaphoreType.REGULAR,
        ]
        + [pltpu.SemaphoreType.DMA] * 12
        + [pltpu.SemaphoreType.DMA((3, 12, 2))] * 2
        + [pltpu.SemaphoreType.DMA((3, 20))] * 2,
        compiler_params=pltpu.CompilerParams(
            collective_id=0, has_side_effects=True, vmem_limit_bytes=40 * 2**20
        ),
        name="step",
    )(outgoing, momentum, mine, slot_index)


def place_kernel(buf, update, sem):
    copies = [
        pltpu.make_async_copy(
            buf.at[j // 16, j // 4 % 4, j % 4], update.at[:, pl.ds(128 * j, 128)], sem.at[j]
        )
        for j in range(TILES)
    ]
    for copy in copies:
        copy.start()
    for copy in copies:
        copy.wait()


def place_tiles(buf):
    return pl.pallas_call(
        place_kernel,
        out_shape=jax.ShapeDtypeStruct((2 * R, 128 * TILES), BF16),
        in_specs=[pl.BlockSpec(memory_space=pl.ANY)],
        out_specs=pl.BlockSpec(memory_space=pl.ANY),
        scratch_shapes=[pltpu.SemaphoreType.DMA((TILES,))],
        compiler_params=pltpu.CompilerParams(vmem_limit_bytes=2 * 2**20),
        name="place",
    )(buf)


def slot_of_blocks(table, slot_count):
    positions = jnp.arange(table.shape[0], dtype=jnp.int32)
    matching = (table[None, :] == table[:, None]) & (positions[None, :] < positions[:, None])
    ranking = jnp.sum(matching.astype(jnp.int32), axis=1)
    return table * slot_count + ranking


def local(grads, momentum, table):
    me = lax.axis_index("dp")
    slot_index = slot_of_blocks(table, 3)
    hits = slot_index[None, :] == jnp.arange(384, dtype=jnp.int32)[:, None]
    count = jnp.sum((table == me).astype(jnp.int32))
    mine = (jnp.arange(3, dtype=jnp.int32) < count).astype(F32)
    pieces = jnp.pad(grads.reshape(9, 128, 56), ((0, 1), (0, 0), (0, 8)))
    pieces = pieces.transpose(1, 0, 2).reshape(128, 640)
    outgoing = jnp.dot(hits.astype(BF16), pieces, preferred_element_type=F32).astype(BF16)
    outgoing = jnp.pad(outgoing.reshape(128, 15, 128), ((0, 0), (0, 1), (0, 0)))
    fresh, buf = step(outgoing, momentum, mine, slot_index)
    return place_tiles(buf), fresh


def solution(mesh):
    in_specs = (P("dp", None), P("dp", None, None), P())
    out_specs = (P(), P("dp", None, None))
    return jax.shard_map(local, mesh=mesh, in_specs=in_specs, out_specs=out_specs, check_vma=False)
```

time: 1120 us -> 148 us (0.13)
  waiting for transfers between devices: 870 us -> 0 us
  Pallas kernels: 0 us -> 139 us
  matrix products: 98 us -> 0.3 us
  blocking collectives: 62.9 us -> 0 us
  local copies, waits for them, and re-layouts: 38.2 us -> 3.91 us
  starting transfers between devices: 19.3 us -> 0 us
  between operations: 14.9 us -> 0.71 us
    psum x5 -> x0, waiting for transfers between devices: 749 us -> none  [gram_sum(): return lax.psum(partial_gram, 'dp')]
    pallas_call x0 -> x2, Pallas kernels: none -> 139 us  [the longest x1 133 us: step(): pl.pallas_call(step_kernel, out_shape=(jax.ShapeDtypeStruct(momentum.shap...]
    all_gather x1 -> x0, waiting for transfers between devices: 96.8 us -> none  [local(): update = lax.all_gather(ordered, 'dp', axis=0, tiled=True)]
    dot_general x10 -> x1, matrix products: 78.9 us -> 0.3 us  [local(): jnp.dot(hits.astype(BF16), pieces, preferred_element_type=F32).astype(BF16)]
    psum x1 -> x0, blocking collectives: 62.9 us -> none  [local(): squares = lax.psum(jnp.sum(per_layer * per_layer, axis=(0, 1, 3)), 'dp')]
    unnamed x18 -> x5, local copies, waits for them, and re-layouts: 29.3 us -> 0.89 us
    all_to_all x2 -> x0, waiting for transfers between devices: 24.4 us -> none  [the longest x1 12.2 us: local(): lax.all_to_all(going_back, 'dp', split_axis=2, concat_axis=0, tiled=True)]
    unnamed x5 -> x0, matrix products: 19.1 us -> none
  transfers between devices with their start and end apart: 8 -> 0, of which waited for: 8 -> 0; matrix products, arithmetic and copies ran while one was open for 0% -> 0% of each run, Pallas kernels for 0% -> 0%
where the time goes in v3:
time: 148 us
  Pallas kernels  139 us (94%)
  local copies, waits for them, and re-layouts  3.91 us (3%)
  other arithmetic  3.36 us (2%)
    pallas_call x1, Pallas kernels, step(): pl.pallas_call(step_kernel, out_shape=(jax.ShapeDtypeStruct(momentum.shap...  133 us
    pallas_call x1, Pallas kernels, place_tiles(): pl.pallas_call(place_kernel, out_shape=jax.ShapeDtypeStruct((2 * R, 128 *...  6.21 us

profile of v3, /device:TPU:1, one launch (start us, length us, event | category | flops | bytes accessed | tf_op | source)
XLA Modules:
  0.0 147.5 jit_solution(5378679019390301547)
XLA Ops:
  0.6 0.9 convert_reduce_fusion
  1.5 1.3 fusion.2
  2.8 0.0 copy-start.1
  2.8 1.2 compare_convert_fusion.mine_ref
  4.0 1.5 %reshape.16 = bf16[9,128,56]{2,1,0:T(8,128)(2,1)S(1)} reshape(bf16[9,7168]{1,0:T(8,128)(2,1)} %param.3) | data formatting | bytes 258048 | tf_op jit(solution)/shard_map/reshape | solution.py:591
  5.5 0.1 pad_bitcast_fusion
  5.6 0.2 copy.6
  5.7 0.3 convolution_convert_fusion
  6.0 0.4 reshape.18
  6.5 0.9 pad.9.out_ref
  7.4 0.0 copy-done.1
  7.4 133.0 %step.1 = (f32[3,56,1152]{2,1,0:T(8,128)}, bf16[4,4,4,1152,128]{4,3,2,1,0:T(8,128)(2,1)S(1)}) custom-call(bf16[128,16,128]{2,1,0:T(8,128)(2,1)} %pad.9.out_ref, f32[3,56,1152]{2,1,0:T(8,128)} %mom_ref.1, f32[3]{0:T(128)} %compare_convert_fusion.mine_ref, s32[128]{0:T(128)} %copy-done.1), custom_call_target="tpu_custom_call" | custom-call | tf_op jit(solution)/shard_map/step/pallas_call | solution.py:507
  140.4 0.0 copy-start
  140.4 6.2 %place.1 = bf16[1152,7168]{1,0:T(8,128)(2,1)} custom-call(bf16[4,4,4,1152,128]{4,3,2,1,0:T(8,128)(2,1)S(1)} %get-tuple-element.4.buf), custom_call_target="tpu_custom_call" | custom-call | tf_op jit(solution)/shard_map/place/pallas_call | solution.py:567
  146.6 0.0 copy-done
  146.6 0.9 copy.8
Async XLA Ops:
  2.8 4.5 %copy-start.1 = (s32[128]{0:T(128)}, s32[128]{0:T(128)S(1)}, u32[]{:S(2)}) copy-start(s32[128]{0:T(128)S(1)} %get-tuple-element.7.slot_ref) | copy-start | bytes 1540
  140.4 6.2 %copy-start = (f32[3,56,1152]{2,1,0:T(8,128)S(1)}, f32[3,56,1152]{2,1,0:T(8,128)}, u32[]{:S(2)}) copy-start(f32[3,56,1152]{2,1,0:T(8,128)} %get-tuple-element.11) | copy-start | bytes 2322436

commit v4 on v3

--- a/solution.py
+++ b/solution.py
@@ -14,7 +14,7 @@
 DEVICES = 128
 CHIPS = 64
 TILES = 56
-RELAYS = 35
+RELAYS = 63
 MESH = pl.DeviceIdType.MESH
 F32 = jnp.float32
 BF16 = jnp.bfloat16
@@ -100,22 +100,42 @@
             gram[128 * s : 128 * s + 128, 128 * b : 128 * b + 128] = block.T
 
 
-def greet_all(me, ready):
+def spread(count, factor, act):
+    for i in range(1, 8):
+        act((i * factor) % count)
+
+    def block(b, carry):
+        for i in range(8):
+            act(jnp.bitwise_and((8 * b + i) * factor, count - 1))
+        return carry
+
+    lax.fori_loop(1, count // 8, block, 0)
+
+
+def greet_all(me):
     barrier = pltpu.get_barrier_semaphore()
-    for i in [*range(1, 16), *range(16, DEVICES, 16)]:
+
+    def greet(mask):
         pl.semaphore_signal(
-            barrier, inc=1, device_id=(jnp.bitwise_xor(me, i),), device_id_type=MESH
+            barrier, inc=1, device_id=(jnp.bitwise_xor(me, mask),), device_id_type=MESH
         )
 
-    def finish():
-        pl.semaphore_wait(barrier, 22)
-        for i in range(16, DEVICES, 16):
-            pl.semaphore_signal(
-                ready, inc=1, device_id=(jnp.bitwise_xor(me, i),), device_id_type=MESH
-            )
-        pl.semaphore_wait(ready, 7)
-
-    return finish
+    spread(DEVICES, 45, greet)
+    pl.semaphore_wait(barrier, DEVICES - 1)
+
+
+def place_at(chip):
+    return {"y": chip // 16, "z": lax.rem(chip // 4, 4), "x": lax.rem(chip, 4)}
+
+
+def shift(at, axis, step):
+    moved = dict(at)
+    moved[axis] = lax.rem(at[axis] + step + 4, 4)
+    return moved
+
+
+def device_at(at, core):
+    return ((at["y"] * 4 + at["z"]) * 4 + at["x"]) * 2 + core
 
 
 def left_form(value, ref):
@@ -156,23 +176,22 @@
 SIDES = ((0, 1), (1, -1))
 
 
-def gather_steps(buf, send, recv, sib_send, sib_recv):
+def gather_steps(buf, send_a, send_b, recv_a, recv_b, sib_send, sib_recv):
     me, chip, core = position()
-    home = {"y": chip // 16, "z": lax.rem(chip // 4, 4), "x": lax.rem(chip, 4)}
+    home = place_at(chip)
     sibling = chip * 2 + 1 - core
     parts = range(3)
 
-    def shift(at, axis, step):
-        moved = dict(at)
-        moved[axis] = lax.rem(at[axis] + step + 4, 4)
-        return moved
-
     def device(at):
-        return ((at["y"] * 4 + at["z"]) * 4 + at["x"]) * 2 + core
+        return device_at(at, core)
 
     def rows_of(part, half):
         row = R * core + 192 * part + (0 if half is None else 96 * half)
         return pl.ds(pl.multiple_of(row, 16), 192 if half is None else 96)
+
+    def tile(part, at):
+        y, z, x = at["y"], at["z"], at["x"]
+        return jnp.logical_or(y < 3, z < 2), 1, 0, lambda n: (y, z, pl.ds(x, n))
 
     def line(part, at):
         y, z, x = at["y"], at["z"], at["x"]
@@ -182,10 +201,6 @@
             return z < 2, 4, 3, lambda n: (pl.ds(0, n), z, x)
         return y < 3, 4, 2, lambda n: (y, pl.ds(0, n), x)
 
-    def tile(part, at):
-        y, z, x = at["y"], at["z"], at["x"]
-        return jnp.logical_or(y < 3, z < 2), 1, 0, lambda n: (y, z, pl.ds(x, n))
-
     def each(spec, act):
         whole, count, fewer, index = spec
 
@@ -206,103 +221,135 @@
 
         each(spec, act)
 
-    def take(spec, sem, half=None):
+    def take(spec, sem, rows=192):
         def act(count, index):
-            drain(buf.at[0, 0, pl.ds(0, count), pl.ds(0, 192 if half is None else 96)], sem)
+            drain(buf.at[0, 0, pl.ds(0, count), pl.ds(0, rows)], sem)
 
         each(spec, act)
+
+    def take_halves(first, second, sem):
+        def outer(m, _):
+            def inner(n, _):
+                drain(buf.at[0, 0, 0, pl.ds(0, 96 * (m + n))], sem)
+
+            each(second, inner)
+            if not second[2]:
+
+                @pl.when(jnp.logical_not(second[0]))
+                def _():
+                    drain(buf.at[0, 0, 0, pl.ds(0, 96 * m)], sem)
+
+        each(first, outer)
+        if not first[2]:
+
+            @pl.when(jnp.logical_and(jnp.logical_not(first[0]), second[0]))
+            def _():
+                drain(buf.at[0, 0, 0, pl.ds(0, 96 * second[1])], sem)
 
     def both(part, k, spec, axis):
         for d, step in SIDES:
-            push(part, spec, send.at[part, k, d], recv.at[part, k, d], device(shift(home, axis, step)))
+            push(part, spec, send_a.at[part, k], recv_a.at[part, k, d], device(shift(home, axis, step)))
 
     def pass_on(part, k, spec, d, axis, step):
-        push(part, spec, send.at[part, k, d], recv.at[part, k, d], device(shift(home, axis, step)), half=d)
-
-    def tell(part, n, spec, half=None):
-        push(part, spec, sib_send.at[part, n], sib_recv.at[part, n], sibling, half=half)
+        push(part, spec, send_b.at[part, k], recv_b.at[part, k], device(shift(home, axis, step)), half=d)
 
     def near(part, axis, step, i):
         return line(part, shift(shift(home, axis, step), ORDERS[part][1], OFFSETS[i]))
+
+    def tell(part, spec):
+        push(part, spec, sib_send, sib_recv, sibling)
+
+    def tell_plane(part, at):
+        y, z, x = at["y"], at["z"], at["x"]
+        every = pl.ds(0, 4)
+        if part == 0:
+            tell(part, (z < 2, 4, 3, lambda n: (pl.ds(0, n), z, every)))
+        elif part == 1:
+            tell(part, (x >= 0, 3, 0, lambda n: (pl.ds(0, n), every, x)))
+            tell(part, (x >= 0, 2, 0, lambda n: (3, pl.ds(0, n), x)))
+        else:
+            tell(part, (y < 3, 4, 2, lambda n: (y, pl.ds(0, n), every)))
 
     def forward(part, i):
         axis = ORDERS[part][2]
         for d, step in SIDES:
             got = near(part, axis, -step, i)
-            take(got, recv.at[part, 4 + i, d])
-            pass_on(part, 8 + i, got, d, axis, step)
-            tell(part, 4 + 2 * i + d, got)
-
-    for p in parts:
-        both(p, 0, tile(p, home), ORDERS[p][0])
-    for p in parts:
-        axis = ORDERS[p][0]
+            take(got, recv_a.at[part, 2 + i, d])
+            pass_on(part, 2 + i, got, d, axis, step)
+
+    for p in parts:
+        own, axis = tile(p, home), ORDERS[p][0]
+        both(p, 0, own, axis)
+        push(p, own, send_a.at[p, 0], recv_b.at[p, 0], device(shift(home, axis, 2)))
+    for p in parts:
+        first, second, _ = ORDERS[p]
         for d, step in SIDES:
-            got = tile(p, shift(home, axis, -step))
-            take(got, recv.at[p, 0, d])
-            pass_on(p, 1, got, d, axis, step)
-    for p in parts:
-        first, second, third = ORDERS[p]
+            take(tile(p, shift(home, first, -step)), recv_a.at[p, 0, d])
+        take(tile(p, shift(home, first, 2)), recv_b.at[p, 0])
+        both(p, 1, line(p, home), second)
+    for p in parts:
+        both(p, 2, line(p, home), ORDERS[p][2])
+    for p in parts:
+        second = ORDERS[p][1]
         for d, step in SIDES:
-            take(tile(p, shift(home, first, 2)), recv.at[p, 1, d], half=d)
-        both(p, 2, line(p, home), second)
-        both(p, 4, line(p, home), third)
-        tell(p, 0, line(p, home))
+            got = line(p, shift(home, second, -step))
+            take(got, recv_a.at[p, 1, d])
+            pass_on(p, 1, got, d, second, step)
     for p in parts:
         _, second, third = ORDERS[p]
         for d, step in SIDES:
-            got = line(p, shift(home, second, -step))
-            take(got, recv.at[p, 2, d])
-            pass_on(p, 3, got, d, second, step)
-            both(p, 5 + d, got, third)
-            tell(p, 1 + d, got)
+            both(p, 3 + d, line(p, shift(home, second, -step)), third)
     for p in parts:
         forward(p, 0)
     for p in parts:
         _, second, third = ORDERS[p]
         got = line(p, shift(home, second, 2))
-        for d, step in SIDES:
-            take(got, recv.at[p, 3, d], half=d)
-        both(p, 7, got, third)
-        tell(p, 3, got)
+        take(got, recv_b.at[p, 1])
+        both(p, 5, got, third)
+    for p in parts:
+        tell_plane(p, home)
     for i in (1, 2, 3):
         for p in parts:
             forward(p, i)
+    for p in parts:
+        for d, step in SIDES:
+            tell_plane(p, shift(home, ORDERS[p][2], -step))
     for i in range(4):
         for p in parts:
             got = near(p, ORDERS[p][2], 2, i)
-            for d, step in SIDES:
-                take(got, recv.at[p, 8 + i, d], half=d)
-                tell(p, 12 + 2 * i + d, got, half=d)
+            take(got, recv_b.at[p, 2 + i])
+            tell(p, got)
 
     for p in parts:
         first, second, third = ORDERS[p]
-        for d, step in SIDES:
-            take(tile(p, home), send.at[p, 0, d])
-            take(tile(p, shift(home, first, -step)), send.at[p, 1, d], half=d)
-            take(line(p, home), send.at[p, 2, d])
-            take(line(p, shift(home, second, -step)), send.at[p, 3, d], half=d)
-            for i in range(4):
-                take(near(p, third, 0, i), send.at[p, 4 + i, d])
-                take(near(p, third, -step, i), send.at[p, 8 + i, d], half=d)
-        for sem in (sib_send, sib_recv):
-            for i in range(4):
-                take(near(p, third, 0, i), sem.at[p, i])
-                for d, step in SIDES:
-                    take(near(p, third, -step, i), sem.at[p, 4 + 2 * i + d])
-                    take(near(p, third, 2, i), sem.at[p, 12 + 2 * i + d], half=d)
+        take(tile(p, home), send_a.at[p, 0], 576)
+        take(line(p, home), send_a.at[p, 1], 384)
+        take_halves(line(p, shift(home, second, -1)), line(p, shift(home, second, 1)), send_b.at[p, 1])
+        for i in range(4):
+            take(near(p, third, 0, i), send_a.at[p, 2 + i], 384)
+            take_halves(near(p, third, -1, i), near(p, third, 1, i), send_b.at[p, 2 + i])
+    for sem in (sib_send, sib_recv):
+        drain(buf.at[pl.ds(0, 3), :, :, pl.ds(0, 672)], sem)
 
 
 def step_kernel(
     out_ref, mom_ref, mine_ref, slot_ref, fresh_ref, buf,
-    got, place, columns, packed, terms, summed, relay, chosen, arrived, mcol,
-    gram, gram2, ga, gb, pbs, ta, xa, ready,
-    a2a_send, a2a_recv, swap_send, swap_recv, rs_send, rs_recv, ag_send, ag_recv,
-    h1_send, h1_recv, h2_send, h2_recv, send, recv, sib_send, sib_recv,
+    got, place, columns, packed, terms, partial, terms2, summed, relay, chosen, arrived, mcol,
+    gram, gram2, ga, gb, pbs, ta, xa,
+    a2a_send, a2a_recv, swap_send, swap_recv, rs1_send, rs2_send, ag1_send, ag2_send,
+    h1_send, h1_recv, h2_send, h2_recv, sib_send, sib_recv,
+    rs1_recv, rs2_recv, ag1_recv, ag2_recv, send_a, send_b, recv_b, recv_a,
 ):
     me, chip, core = position()
-    greeted = greet_all(me, ready)
-
+    greet_all(me)
+
+
+    def push(mask):
+        to = jnp.bitwise_xor(me, mask)
+        remote(out_ref.at[to], got.at[me], a2a_send, a2a_recv, to).start()
+
+    spread(DEVICES, 45, push)
+    got[pl.ds(me, 1)] = out_ref[pl.ds(me, 1)]
     rows = lax.broadcasted_iota(jnp.int32, (256, 128), 0)
     lanes = lax.broadcasted_iota(jnp.int32, (1, 128), 1)
     for t in range(9):
@@ -318,16 +365,7 @@
                 place[t, :, pl.ds(128 * (2 * k + parity), 128)] = jnp.where(
                     rows == target, 1.0, 0.0
                 ).astype(BF16)
-    greeted()
-
-    def push(i, carry):
-        to = jnp.bitwise_xor(me, i)
-        remote(out_ref.at[to], got.at[me], a2a_send, a2a_recv, to).start()
-        return carry
-
-    lax.fori_loop(1, DEVICES, push, 0)
-    got[pl.ds(me, 1)] = out_ref[pl.ds(me, 1)]
-    for i in range(ITERS):
+    for i in range(ITERS - 1):
         pbs[i, 1728:K3, :] = jnp.zeros((K3 - 1728, RP), BF16)
     gb[1728:K3, :] = jnp.zeros((K3 - 1728, RP), BF16)
     chosen[DEVICES : DEVICES + 2] = jnp.zeros((2, 8, 128), F32)
@@ -364,33 +402,65 @@
     )[0:R]
     pack(gram, packed)
 
-    def share(c):
-        return pl.ds(pl.multiple_of(24 * c, 8), 24)
-
-    def reduce_push(i, carry):
-        to = jnp.bitwise_xor(chip, i)
-        remote(packed.at[share(to)], terms.at[chip], rs_send, rs_recv, to * 2 + core).start()
-        return carry
-
-    lax.fori_loop(1, CHIPS, reduce_push, 0)
-    terms[pl.ds(chip, 1)] = packed[share(chip)][None]
-    drain(terms.at[pl.ds(0, CHIPS - 1)], rs_recv)
-    summed[share(chip)] = jnp.sum(terms[...], axis=0)
-
-    def gather_push(i, carry):
-        to = jnp.bitwise_xor(chip, i)
-        part = summed.at[share(chip)]
-        remote(part, part, ag_send, ag_recv, to * 2 + core).start()
-        return carry
-
-    lax.fori_loop(1, CHIPS, gather_push, 0)
+    home = place_at(chip)
+
+    def plane_of(p):
+        return home[ORDERS[p][0]] * 4 + home[ORDERS[p][1]]
+
+    def block_of(p, third):
+        return pl.ds(pl.multiple_of(512 * p + 128 * third, 8), 128)
+
+    def piece_of(p, plane):
+        return pl.ds(pl.multiple_of(512 * p + 128 * home[ORDERS[p][2]] + 8 * plane, 8), 8)
+
+    def plane_peer(p, mask):
+        other = jnp.bitwise_xor(plane_of(p), mask)
+        at = dict(home)
+        at[ORDERS[p][0]] = other // 4
+        at[ORDERS[p][1]] = lax.rem(other, 4)
+        return other, device_at(at, core)
+
+    for p in range(3):
+        third = ORDERS[p][2]
+        for step in (1, 2, 3):
+            there = shift(home, third, step)
+            remote(
+                packed.at[block_of(p, there[third])],
+                terms.at[p, home[third]],
+                rs1_send, rs1_recv.at[p], device_at(there, core),
+            ).start()
+    for p in range(3):
+        third = home[ORDERS[p][2]]
+        terms[p, pl.ds(third, 1)] = packed[block_of(p, third)][None]
+        drain(packed.at[pl.ds(0, 384)], rs1_recv.at[p])
+        partial[p] = jnp.sum(terms[p], axis=0)
+        for mask in range(1, 16):
+            other, to = plane_peer(p, mask)
+            remote(
+                partial.at[p, pl.ds(pl.multiple_of(8 * other, 8), 8)],
+                terms2.at[p, plane_of(p)],
+                rs2_send, rs2_recv.at[p], to,
+            ).start()
+    for p in range(3):
+        plane = plane_of(p)
+        terms2[p, pl.ds(plane, 1)] = partial[p, pl.ds(pl.multiple_of(8 * plane, 8), 8)][None]
+        drain(packed.at[pl.ds(0, 120)], rs2_recv.at[p])
+        summed[piece_of(p, plane)] = jnp.sum(terms2[p], axis=0)
+        for mask in range(1, 16):
+            _, to = plane_peer(p, mask)
+            piece = summed.at[piece_of(p, plane)]
+            remote(piece, piece, ag1_send, ag1_recv.at[p], to).start()
+    for p in range(3):
+        third = ORDERS[p][2]
+        drain(packed.at[pl.ds(0, 120)], ag1_recv.at[p])
+        block = summed.at[block_of(p, home[third])]
+        for step in (1, 2, 3):
+            remote(block, block, ag2_send, ag2_recv.at[p], device_at(shift(home, third, step), core)).start()
 
     def to_relay(i, carry):
-        layer = i // RELAYS
-        u = lax.rem(i, RELAYS)
-        t = u // 7 + 4 * layer
-        q = lax.rem(u, 7)
-        to = jnp.where(layer == 0, u * 2 + 1, (63 - u) * 2)
+        t = i // 7
+        q = lax.rem(i, 7)
+        to = jnp.where(i < 28, 2 * i + 1, jnp.where(i < 35, 2 * i + 57, 2 * i - 14))
         src = fresh_ref.at[
             :, pl.ds(pl.multiple_of(8 * q, 8), 8), pl.ds(pl.multiple_of(128 * t, 128), 128)
         ]
@@ -406,9 +476,10 @@
 
         return carry
 
-    lax.fori_loop(0, 2 * RELAYS, to_relay, 0)
-
-    drain(summed.at[pl.ds(0, 24 * (CHIPS - 1))], ag_recv)
+    lax.fori_loop(0, RELAYS, to_relay, 0, unroll=7)
+
+    for p in range(3):
+        drain(packed.at[pl.ds(0, 384)], ag2_recv.at[p])
     unpack(summed, gram)
     diag = lax.broadcasted_iota(jnp.int32, (R, RP), 0) == lax.broadcasted_iota(jnp.int32, (R, RP), 1)
     squares = jnp.sum(jnp.where(diag, gram[...], 0.0), axis=(0, 1), keepdims=True)
@@ -432,15 +503,17 @@
 
     lax.fori_loop(0, 2, sweep, 0)
 
-    layer = 1 - core
-    u = jnp.where(layer == 0, chip, 63 - chip)
-    lane_tile = u // 7
+    spans = jnp.logical_and(core == 1, jnp.logical_and(chip >= 56, chip < 63))
+    sole = jnp.where(core == 1, chip < 28, jnp.logical_and(chip >= 28, chip < 56))
+    relays = jnp.logical_or(spans, sole)
+    u = jnp.where(core == 1, jnp.where(chip < 28, chip, chip - 28), chip + 7)
+    lane_tile = u // 7 - 4 * (1 - core)
     q = lax.rem(u, 7)
 
     def first_block(j, q):
         return (16 * j - q + 6) // 7
 
-    @pl.when(u < RELAYS)
+    @pl.when(relays)
     def _():
         drain(relay, h1_recv)
 
@@ -452,13 +525,22 @@
 
         def to_columns(j, carry):
             src = chosen.at[pl.ds(first_block(j, q), 3)]
-            remote(src, arrived.at[lane_tile, q], h2_send, h2_recv, j * 2 + layer).start()
+            remote(src, arrived.at[lane_tile, q], h2_send, h2_recv, j * 2 + 1 - core).start()
             return carry
 
-        lax.fori_loop(0, TILES, to_columns, 0)
+        lax.fori_loop(0, TILES, to_columns, 0, unroll=8)
+
+        @pl.when(spans)
+        def _():
+            def to_others(j, carry):
+                src = chosen.at[pl.ds(first_block(j, q), 3)]
+                remote(src, arrived.at[0, q], h2_send, h2_recv, j * 2 + 1).start()
+                return carry
+
+            lax.fori_loop(0, TILES, to_others, 0, unroll=8)
 
     lax.fori_loop(2, ITERS - 1, sweep, 0)
-    polynomial(ITERS - 1)
+    right_form(gram[...], gb)
 
     @pl.when(chip < TILES)
     def _():
@@ -482,32 +564,46 @@
         left_form(value, xa)
         return dot(xa[...], pbs[i])
 
-    value = lax.fori_loop(0, ITERS, apply, value) * (0.2 * math.sqrt(max(R, 7168)))
+    value = lax.fori_loop(0, ITERS - 1, apply, value)
+    left_form(value, xa)
+    once = dot(xa[...], gb[...])
+    left_form(once, xa)
+    twice = dot(xa[...], gb[...])
+    value = (coef_a * value + coef_b * once + coef_c * twice) * (0.2 * math.sqrt(max(R, 7168)))
     buf[chip // 16, lax.rem(chip // 4, 4), lax.rem(chip, 4), pl.ds(pl.multiple_of(R * core, 16), R)] = (
         value.T[0:R, :].astype(BF16)
     )
-    gather_steps(buf, send, recv, sib_send, sib_recv)
+    gather_steps(buf, send_a, send_b, recv_a, recv_b, sib_send, sib_recv)
 
     drain(others, a2a_send)
     swap.wait_send()
-    drain(terms.at[pl.ds(0, CHIPS - 1)], rs_send)
-    drain(summed.at[pl.ds(0, 24 * (CHIPS - 1))], ag_send)
-
-    @pl.when(u < RELAYS)
+    drain(packed.at[pl.ds(0, 1152)], rs1_send)
+    drain(packed.at[pl.ds(0, 360)], rs2_send)
+    drain(packed.at[pl.ds(0, 360)], ag1_send)
+    drain(packed.at[pl.ds(0, 1152)], ag2_send)
+
+    @pl.when(relays)
     def _():
-        drain(relay.at[pl.ds(0, 3 * (2 * RELAYS - 1))], h1_send)
+        drain(relay.at[pl.ds(0, 3 * (RELAYS - 1))], h1_send)
+
+    @pl.when(jnp.logical_not(relays))
+    def _():
+        drain(relay.at[pl.ds(0, 3 * RELAYS)], h1_send)
+
+    @pl.when(sole)
+    def _():
         drain(relay.at[pl.ds(0, 3 * TILES)], h2_send)
 
-    @pl.when(u >= RELAYS)
+    @pl.when(spans)
     def _():
-        drain(relay.at[pl.ds(0, 3 * 2 * RELAYS)], h1_send)
+        drain(relay.at[pl.ds(0, 6 * TILES)], h2_send)
 
 
 def step(outgoing, momentum, mine, slot_index):
     return pl.pallas_call(
         step_kernel,
         out_shape=(
-            jax.ShapeDtypeStruct(momentum.shape, F32),
+            pltpu.VMEM(momentum.shape, F32),
             pltpu.VMEM((4, 4, 4, 2 * R, 128), BF16),
         ),
         in_specs=[
@@ -525,7 +621,9 @@
             pltpu.VMEM((9, 256, 768), BF16),
             pltpu.VMEM((2, 3, 56, RP), F32),
             pltpu.VMEM((1536, 128), F32),
-            pltpu.VMEM((CHIPS, 24, 128), F32),
+            pltpu.VMEM((3, 4, 128, 128), F32),
+            pltpu.VMEM((3, 128, 128), F32),
+            pltpu.VMEM((3, 16, 8, 128), F32),
             pltpu.VMEM((1536, 128), F32),
             pltpu.VMEM((384, 8, 128), F32),
             pltpu.VMEM((DEVICES + 2, 8, 128), F32),
@@ -535,14 +633,14 @@
             pltpu.VMEM((R, RP), F32),
             pltpu.VMEM((R, K3), BF16),
             pltpu.VMEM((K3, RP), BF16),
-            pltpu.VMEM((ITERS, K3, RP), BF16),
+            pltpu.VMEM((ITERS - 1, K3, RP), BF16),
             pltpu.VMEM((R, K3), BF16),
             pltpu.VMEM((128, K3), BF16),
-            pltpu.SemaphoreType.REGULAR,
         ]
-        + [pltpu.SemaphoreType.DMA] * 12
-        + [pltpu.SemaphoreType.DMA((3, 12, 2))] * 2
-        + [pltpu.SemaphoreType.DMA((3, 20))] * 2,
+        + [pltpu.SemaphoreType.DMA] * 14
+        + [pltpu.SemaphoreType.DMA((3,))] * 4
+        + [pltpu.SemaphoreType.DMA((3, 6))] * 3
+        + [pltpu.SemaphoreType.DMA((3, 6, 2))],
         compiler_params=pltpu.CompilerParams(
             collective_id=0, has_side_effects=True, vmem_limit_bytes=40 * 2**20
         ),
@@ -550,29 +648,33 @@
     )(outgoing, momentum, mine, slot_index)
 
 
-def place_kernel(buf, update, sem):
+def place_kernel(buf, fresh, update, momentum, sem):
     copies = [
         pltpu.make_async_copy(
             buf.at[j // 16, j // 4 % 4, j % 4], update.at[:, pl.ds(128 * j, 128)], sem.at[j]
         )
         for j in range(TILES)
     ]
+    copies.append(pltpu.make_async_copy(fresh, momentum, sem.at[TILES]))
     for copy in copies:
         copy.start()
     for copy in copies:
         copy.wait()
 
 
-def place_tiles(buf):
+def place_results(buf, fresh):
     return pl.pallas_call(
         place_kernel,
-        out_shape=jax.ShapeDtypeStruct((2 * R, 128 * TILES), BF16),
-        in_specs=[pl.BlockSpec(memory_space=pl.ANY)],
-        out_specs=pl.BlockSpec(memory_space=pl.ANY),
-        scratch_shapes=[pltpu.SemaphoreType.DMA((TILES,))],
+        out_shape=(
+            jax.ShapeDtypeStruct((2 * R, 128 * TILES), BF16),
+            jax.ShapeDtypeStruct(fresh.shape, F32),
+        ),
+        in_specs=[pl.BlockSpec(memory_space=pl.ANY)] * 2,
+        out_specs=(pl.BlockSpec(memory_space=pl.ANY),) * 2,
+        scratch_shapes=[pltpu.SemaphoreType.DMA((TILES + 1,))],
         compiler_params=pltpu.CompilerParams(vmem_limit_bytes=2 * 2**20),
         name="place",
-    )(buf)
+    )(buf, fresh)
 
 
 def slot_of_blocks(table, slot_count):
@@ -593,7 +695,7 @@
     outgoing = jnp.dot(hits.astype(BF16), pieces, preferred_element_type=F32).astype(BF16)
     outgoing = jnp.pad(outgoing.reshape(128, 15, 128), ((0, 0), (0, 1), (0, 0)))
     fresh, buf = step(outgoing, momentum, mine, slot_index)
-    return place_tiles(buf), fresh
+    return place_results(buf, fresh)
 
 
 def solution(mesh):

time: 148 us -> 129 us (0.87)
  Pallas kernels: 139 us -> 121 us
    pallas_call x2, Pallas kernels: 139 us -> 121 us  [the longest x1 115 us: step(): pl.pallas_call(step_kernel, out_shape=(pltpu.VMEM(momentum.shape, F32), p...]
where the time goes in v4:
time: 129 us
  Pallas kernels  121 us (94%)
  other arithmetic  3.36 us (3%)
  local copies, waits for them, and re-layouts  3.03 us (2%)
    pallas_call x1, Pallas kernels, step(): pl.pallas_call(step_kernel, out_shape=(pltpu.VMEM(momentum.shape, F32), p...  115 us
    pallas_call x1, Pallas kernels, place_results(): pl.pallas_call(place_kernel, out_shape=(jax.ShapeDtypeStruct((2 * R, 128...  6.47 us

profile of v4, /device:TPU:1, one launch (start us, length us, event | category | flops | bytes accessed | tf_op | source)
XLA Modules:
  0.0 128.8 jit_solution(17318856385661122736)
XLA Ops:
  0.6 0.9 convert_reduce_fusion
  1.5 1.3 %fusion.2 = (s32[]{:T(128)}, s32[128]{0:T(128)S(1)}) fusion(s32[128]{0:T(128)} %param.5, s32[]{:T(128)S(6)} %axis_index.12, s32[128]{0:T(128)S(1)} %convert_reduce_fusion), kind=kLoop, calls=%fused_computation.9 | loop fusion | flops 639 | bytes 1544 | tf_op jit(solution)/shard_map/reduce_sum | solution.py:691
  2.8 0.0 copy-start
  2.8 1.2 compare_convert_fusion.mine_ref
  4.0 1.5 %reshape.16 = bf16[9,128,56]{2,1,0:T(8,128)(2,1)S(1)} reshape(bf16[9,7168]{1,0:T(8,128)(2,1)} %param.3) | data formatting | bytes 258048 | tf_op jit(solution)/shard_map/reshape | solution.py:693
  5.5 0.1 pad_bitcast_fusion
  5.6 0.2 copy.6
  5.7 0.3 convolution_convert_fusion
  6.0 0.4 reshape.18
  6.5 0.9 pad.9.out_ref
  7.4 0.0 copy-done
  7.4 114.8 %step.1 = (f32[3,56,1152]{2,1,0:T(8,128)S(1)}, bf16[4,4,4,1152,128]{4,3,2,1,0:T(8,128)(2,1)S(1)}) custom-call(bf16[128,16,128]{2,1,0:T(8,128)(2,1)} %pad.9.out_ref, f32[3,56,1152]{2,1,0:T(8,128)} %mom_ref.1, f32[3]{0:T(128)} %compare_convert_fusion.mine_ref, s32[128]{0:T(128)} %copy-done), custom_call_target="tpu_custom_call" | custom-call | tf_op jit(solution)/shard_map/step/pallas_call | solution.py:603
  122.1 6.5 %place.1 = (bf16[1152,7168]{1,0:T(8,128)(2,1)}, f32[3,56,1152]{2,1,0:T(8,128)}) custom-call(bf16[4,4,4,1152,128]{4,3,2,1,0:T(8,128)(2,1)S(1)} %get-tuple-element.4.buf, f32[3,56,1152]{2,1,0:T(8,128)S(1)} %get-tuple-element.5.fresh), custom_call_target="tpu_custom_call" | custom-call | tf_op jit(solution)/shard_map/place/pallas_call | solution.py:666
Async XLA Ops:
  2.8 4.5 %copy-start = (s32[128]{0:T(128)}, s32[128]{0:T(128)S(1)}, u32[]{:S(2)}) copy-start(s32[128]{0:T(128)S(1)} %get-tuple-element.7.slot_ref) | copy-start | bytes 1540

commit v5 on v4

--- a/solution.py
+++ b/solution.py
@@ -121,7 +121,7 @@
         )
 
     spread(DEVICES, 45, greet)
-    pl.semaphore_wait(barrier, DEVICES - 1)
+    return lambda: pl.semaphore_wait(barrier, DEVICES - 1)
 
 
 def place_at(chip):
@@ -333,23 +333,41 @@
 
 
 def step_kernel(
-    out_ref, mom_ref, mine_ref, slot_ref, fresh_ref, buf,
-    got, place, columns, packed, terms, partial, terms2, summed, relay, chosen, arrived, mcol,
+    pieces_ref, mom_ref, table_ref, fresh_ref, buf,
+    hits, outgoing, slot_row, slots, got, place, columns, packed, terms, partial, terms2, summed, relay, chosen, arrived, mcol,
     gram, gram2, ga, gb, pbs, ta, xa,
     a2a_send, a2a_recv, swap_send, swap_recv, rs1_send, rs2_send, ag1_send, ag2_send,
-    h1_send, h1_recv, h2_send, h2_recv, sib_send, sib_recv,
+    h1_send, h1_recv, h2_send, h2_recv, sib_send, sib_recv, slot_sem,
     rs1_recv, rs2_recv, ag1_recv, ag2_recv, send_a, send_b, recv_b, recv_a,
 ):
     me, chip, core = position()
-    greet_all(me)
+    greeted = greet_all(me)
+
+    table = table_ref[...].astype(F32)
+    owners = jnp.broadcast_to(table, (DEVICES, DEVICES))
+    sub = lax.broadcasted_iota(jnp.int32, (DEVICES, DEVICES), 0)
+    lane = lax.broadcasted_iota(jnp.int32, (DEVICES, DEVICES), 1)
+    earlier = jnp.logical_and(owners == owners.T, sub < lane)
+    rank = jnp.sum(jnp.where(earlier, 1.0, 0.0), axis=0, keepdims=True)
+    slot_row[...] = (3.0 * table + rank).astype(jnp.int32)
+    slot_copy = pltpu.make_async_copy(slot_row, slots, slot_sem)
+    slot_copy.start()
+    owned = jnp.sum(jnp.where(table == me.astype(F32), 1.0, 0.0), axis=1, keepdims=True)
+    line = (16.0 * table + 5.0 * rank).astype(jnp.int32)
+    lines = lax.broadcasted_iota(jnp.int32, (16 * DEVICES, DEVICES), 0)
+    for i in range(5):
+        hits[:, 128 * i : 128 * i + 128] = jnp.where(lines == line + i, 1.0, 0.0).astype(BF16)
+    outgoing[...] = dot(hits[...], pieces_ref[...]).astype(BF16).reshape(DEVICES, 16, 128)
+    slot_copy.wait()
+    greeted()
 
 
     def push(mask):
         to = jnp.bitwise_xor(me, mask)
-        remote(out_ref.at[to], got.at[me], a2a_send, a2a_recv, to).start()
+        remote(outgoing.at[to], got.at[me], a2a_send, a2a_recv, to).start()
 
     spread(DEVICES, 45, push)
-    got[pl.ds(me, 1)] = out_ref[pl.ds(me, 1)]
+    got[pl.ds(me, 1)] = outgoing[pl.ds(me, 1)]
     rows = lax.broadcasted_iota(jnp.int32, (256, 128), 0)
     lanes = lax.broadcasted_iota(jnp.int32, (1, 128), 1)
     for t in range(9):
@@ -383,7 +401,7 @@
             )
             fresh_ref[k, :, pl.ds(128 * t, 128)] = (
                 0.95 * mom_ref[k, :, pl.ds(128 * t, 128)] + grad
-            ) * mine_ref[k]
+            ) * jnp.where(owned > k, 1.0, 0.0)
 
     sibling = chip * 2 + 1 - core
     mine_lanes = pl.ds(pl.multiple_of(512 * core, 128), RP)
@@ -457,7 +475,8 @@
         for step in (1, 2, 3):
             remote(block, block, ag2_send, ag2_recv.at[p], device_at(shift(home, third, step), core)).start()
 
-    def to_relay(i, carry):
+    def to_relay(n, carry):
+        i = lax.rem(n + 28, RELAYS)
         t = i // 7
         q = lax.rem(i, 7)
         to = jnp.where(i < 28, 2 * i + 1, jnp.where(i < 35, 2 * i + 57, 2 * i - 14))
@@ -481,6 +500,39 @@
     for p in range(3):
         drain(packed.at[pl.ds(0, 384)], ag2_recv.at[p])
     unpack(summed, gram)
+    spans = jnp.logical_and(core == 1, jnp.logical_and(chip >= 56, chip < 63))
+    sole = jnp.where(core == 1, chip < 28, jnp.logical_and(chip >= 28, chip < 56))
+    relays = jnp.logical_or(spans, sole)
+    u = jnp.where(core == 1, jnp.where(chip < 28, chip, chip - 28), chip + 7)
+    lane_tile = u // 7 - 4 * (1 - core)
+    q = lax.rem(u, 7)
+
+    def first_block(j, q):
+        return (16 * j - q + 6) // 7
+
+    def relay_blocks():
+        drain(relay, h1_recv)
+
+        def choose(b, carry):
+            chosen[pl.ds(b, 1)] = relay[pl.ds(jnp.clip(slots[0, b], 0, 383), 1)]
+            return carry
+
+        lax.fori_loop(0, DEVICES, choose, 0, unroll=8)
+
+    def send_columns(tile, layer):
+        def to_columns(j, carry):
+            src = chosen.at[pl.ds(first_block(j, q), 3)]
+            remote(src, arrived.at[tile, q], h2_send, h2_recv, j * 2 + layer).start()
+            return carry
+
+        lax.fori_loop(0, TILES, to_columns, 0, unroll=8)
+
+    @pl.when(spans)
+    def _():
+        relay_blocks()
+        send_columns(4, 0)
+        send_columns(0, 1)
+
     diag = lax.broadcasted_iota(jnp.int32, (R, RP), 0) == lax.broadcasted_iota(jnp.int32, (R, RP), 1)
     squares = jnp.sum(jnp.where(diag, gram[...], 0.0), axis=(0, 1), keepdims=True)
     inverse = 1.0 / (jnp.sqrt(squares) + epsilon)
@@ -503,41 +555,10 @@
 
     lax.fori_loop(0, 2, sweep, 0)
 
-    spans = jnp.logical_and(core == 1, jnp.logical_and(chip >= 56, chip < 63))
-    sole = jnp.where(core == 1, chip < 28, jnp.logical_and(chip >= 28, chip < 56))
-    relays = jnp.logical_or(spans, sole)
-    u = jnp.where(core == 1, jnp.where(chip < 28, chip, chip - 28), chip + 7)
-    lane_tile = u // 7 - 4 * (1 - core)
-    q = lax.rem(u, 7)
-
-    def first_block(j, q):
-        return (16 * j - q + 6) // 7
-
-    @pl.when(relays)
+    @pl.when(sole)
     def _():
-        drain(relay, h1_recv)
-
-        def choose(b, carry):
-            chosen[pl.ds(b, 1)] = relay[pl.ds(slot_ref[b], 1)]
-            return carry
-
-        lax.fori_loop(0, DEVICES, choose, 0, unroll=8)
-
-        def to_columns(j, carry):
-            src = chosen.at[pl.ds(first_block(j, q), 3)]
-            remote(src, arrived.at[lane_tile, q], h2_send, h2_recv, j * 2 + 1 - core).start()
-            return carry
-
-        lax.fori_loop(0, TILES, to_columns, 0, unroll=8)
-
-        @pl.when(spans)
-        def _():
-            def to_others(j, carry):
-                src = chosen.at[pl.ds(first_block(j, q), 3)]
-                remote(src, arrived.at[0, q], h2_send, h2_recv, j * 2 + 1).start()
-                return carry
-
-            lax.fori_loop(0, TILES, to_others, 0, unroll=8)
+        relay_blocks()
+        send_columns(lane_tile, 1 - core)
 
     lax.fori_loop(2, ITERS - 1, sweep, 0)
     right_form(gram[...], gb)
@@ -599,7 +620,7 @@
         drain(relay.at[pl.ds(0, 6 * TILES)], h2_send)
 
 
-def step(outgoing, momentum, mine, slot_index):
+def step(pieces, momentum, table):
     return pl.pallas_call(
         step_kernel,
         out_shape=(
@@ -609,14 +630,17 @@
         in_specs=[
             pl.BlockSpec(memory_space=pltpu.VMEM),
             pl.BlockSpec(memory_space=pltpu.VMEM),
-            pl.BlockSpec(memory_space=pltpu.SMEM),
-            pl.BlockSpec(memory_space=pltpu.SMEM),
+            pl.BlockSpec(memory_space=pltpu.VMEM),
         ],
         out_specs=(
             pl.BlockSpec(memory_space=pltpu.VMEM),
             pl.BlockSpec(memory_space=pltpu.VMEM),
         ),
         scratch_shapes=[
+            pltpu.VMEM((16 * DEVICES, 5 * 128), BF16),
+            pltpu.VMEM((DEVICES, 16, 128), BF16),
+            pltpu.VMEM((1, DEVICES), jnp.int32),
+            pltpu.SMEM((1, DEVICES), jnp.int32),
             pltpu.VMEM((DEVICES, 16, 128), BF16),
             pltpu.VMEM((9, 256, 768), BF16),
             pltpu.VMEM((2, 3, 56, RP), F32),
@@ -637,7 +661,7 @@
             pltpu.VMEM((R, K3), BF16),
             pltpu.VMEM((128, K3), BF16),
         ]
-        + [pltpu.SemaphoreType.DMA] * 14
+        + [pltpu.SemaphoreType.DMA] * 15
         + [pltpu.SemaphoreType.DMA((3,))] * 4
         + [pltpu.SemaphoreType.DMA((3, 6))] * 3
         + [pltpu.SemaphoreType.DMA((3, 6, 2))],
@@ -645,7 +669,7 @@
             collective_id=0, has_side_effects=True, vmem_limit_bytes=40 * 2**20
         ),
         name="step",
-    )(outgoing, momentum, mine, slot_index)
+    )(pieces, momentum, table)
 
 
 def place_kernel(buf, fresh, update, momentum, sem):
@@ -677,24 +701,10 @@
     )(buf, fresh)
 
 
-def slot_of_blocks(table, slot_count):
-    positions = jnp.arange(table.shape[0], dtype=jnp.int32)
-    matching = (table[None, :] == table[:, None]) & (positions[None, :] < positions[:, None])
-    ranking = jnp.sum(matching.astype(jnp.int32), axis=1)
-    return table * slot_count + ranking
-
-
 def local(grads, momentum, table):
-    me = lax.axis_index("dp")
-    slot_index = slot_of_blocks(table, 3)
-    hits = slot_index[None, :] == jnp.arange(384, dtype=jnp.int32)[:, None]
-    count = jnp.sum((table == me).astype(jnp.int32))
-    mine = (jnp.arange(3, dtype=jnp.int32) < count).astype(F32)
     pieces = jnp.pad(grads.reshape(9, 128, 56), ((0, 1), (0, 0), (0, 8)))
-    pieces = pieces.transpose(1, 0, 2).reshape(128, 640)
-    outgoing = jnp.dot(hits.astype(BF16), pieces, preferred_element_type=F32).astype(BF16)
-    outgoing = jnp.pad(outgoing.reshape(128, 15, 128), ((0, 0), (0, 1), (0, 0)))
-    fresh, buf = step(outgoing, momentum, mine, slot_index)
+    pieces = pieces.reshape(5, 2, 128, 64).transpose(0, 2, 1, 3).reshape(640, 128)
+    fresh, buf = step(pieces, momentum, table.reshape(1, DEVICES))
     return place_results(buf, fresh)
 
 

time: 129 us -> 126 us (0.977)
  other arithmetic: 3.36 us -> 0 us
    reduce_sum x2 -> x0, other arithmetic: 2.2 us -> none  [the longest x1 1.3 us: local(): count = jnp.sum((table == me).astype(jnp.int32))]
where the time goes in v5:
time: 126 us
  Pallas kernels  122 us (97%)
  local copies, waits for them, and re-layouts  2.73 us (2%)
    pallas_call x1, Pallas kernels, step(): pl.pallas_call(step_kernel, out_shape=(pltpu.VMEM(momentum.shape, F32), p...  116 us
    pallas_call x1, Pallas kernels, place_results(): pl.pallas_call(place_kernel, out_shape=(jax.ShapeDtypeStruct((2 * R, 128...  6.47 us

profile of v5, /device:TPU:1, one launch (start us, length us, event | category | flops | bytes accessed | tf_op | source)
XLA Modules:
  0.0 125.6 jit_solution(9620125755200225967)
XLA Ops:
  0.6 1.5 %reshape.16 = bf16[9,128,56]{2,1,0:T(8,128)(2,1)S(1)} reshape(bf16[9,7168]{1,0:T(8,128)(2,1)} %param.3) | data formatting | bytes 258048 | tf_op jit(solution)/shard_map/reshape | solution.py:705
  2.1 0.1 pad.4
  2.2 0.3 copy.9
  2.5 0.8 reshape.20.pieces_ref
  3.4 115.6 %step.1 = (f32[3,56,1152]{2,1,0:T(8,128)S(1)}, bf16[4,4,4,1152,128]{4,3,2,1,0:T(8,128)(2,1)S(1)}) custom-call(bf16[640,128]{1,0:T(8,128)(2,1)} %reshape.20.pieces_ref, f32[3,56,1152]{2,1,0:T(8,128)} %mom_ref.1, s32[1,128]{1,0:T(1,128)} %bitcast.5), custom_call_target="tpu_custom_call" | custom-call | tf_op jit(solution)/shard_map/step/pallas_call | solution.py:624
  119.0 6.5 %place.1 = (bf16[1152,7168]{1,0:T(8,128)(2,1)}, f32[3,56,1152]{2,1,0:T(8,128)}) custom-call(bf16[4,4,4,1152,128]{4,3,2,1,0:T(8,128)(2,1)S(1)} %get-tuple-element.4.buf, f32[3,56,1152]{2,1,0:T(8,128)S(1)} %get-tuple-element.5.fresh), custom_call_target="tpu_custom_call" | custom-call | tf_op jit(solution)/shard_map/place/pallas_call | solution.py:690

commit v6 on v5

--- a/solution.py
+++ b/solution.py
@@ -176,7 +176,7 @@
 SIDES = ((0, 1), (1, -1))
 
 
-def gather_steps(buf, send_a, send_b, recv_a, recv_b, sib_send, sib_recv):
+def gather_steps(buf, send_a, send_b, recv_a, recv_b, sib_send, sib_recv, meanwhile):
     me, chip, core = position()
     home = place_at(chip)
     sibling = chip * 2 + 1 - core
@@ -259,28 +259,19 @@
     def tell(part, spec):
         push(part, spec, sib_send, sib_recv, sibling)
 
-    def tell_plane(part, at):
-        y, z, x = at["y"], at["z"], at["x"]
-        every = pl.ds(0, 4)
-        if part == 0:
-            tell(part, (z < 2, 4, 3, lambda n: (pl.ds(0, n), z, every)))
-        elif part == 1:
-            tell(part, (x >= 0, 3, 0, lambda n: (pl.ds(0, n), every, x)))
-            tell(part, (x >= 0, 2, 0, lambda n: (3, pl.ds(0, n), x)))
-        else:
-            tell(part, (y < 3, 4, 2, lambda n: (y, pl.ds(0, n), every)))
-
     def forward(part, i):
         axis = ORDERS[part][2]
         for d, step in SIDES:
             got = near(part, axis, -step, i)
             take(got, recv_a.at[part, 2 + i, d])
             pass_on(part, 2 + i, got, d, axis, step)
+            tell(part, got)
 
     for p in parts:
         own, axis = tile(p, home), ORDERS[p][0]
         both(p, 0, own, axis)
         push(p, own, send_a.at[p, 0], recv_b.at[p, 0], device(shift(home, axis, 2)))
+    meanwhile()
     for p in parts:
         first, second, _ = ORDERS[p]
         for d, step in SIDES:
@@ -289,6 +280,7 @@
         both(p, 1, line(p, home), second)
     for p in parts:
         both(p, 2, line(p, home), ORDERS[p][2])
+        tell(p, line(p, home))
     for p in parts:
         second = ORDERS[p][1]
         for d, step in SIDES:
@@ -298,7 +290,9 @@
     for p in parts:
         _, second, third = ORDERS[p]
         for d, step in SIDES:
-            both(p, 3 + d, line(p, shift(home, second, -step)), third)
+            got = line(p, shift(home, second, -step))
+            both(p, 3 + d, got, third)
+            tell(p, got)
     for p in parts:
         forward(p, 0)
     for p in parts:
@@ -306,20 +300,10 @@
         got = line(p, shift(home, second, 2))
         take(got, recv_b.at[p, 1])
         both(p, 5, got, third)
-    for p in parts:
-        tell_plane(p, home)
+        tell(p, got)
     for i in (1, 2, 3):
         for p in parts:
             forward(p, i)
-    for p in parts:
-        for d, step in SIDES:
-            tell_plane(p, shift(home, ORDERS[p][2], -step))
-    for i in range(4):
-        for p in parts:
-            got = near(p, ORDERS[p][2], 2, i)
-            take(got, recv_b.at[p, 2 + i])
-            tell(p, got)
-
     for p in parts:
         first, second, third = ORDERS[p]
         take(tile(p, home), send_a.at[p, 0], 576)
@@ -327,14 +311,23 @@
         take_halves(line(p, shift(home, second, -1)), line(p, shift(home, second, 1)), send_b.at[p, 1])
         for i in range(4):
             take(near(p, third, 0, i), send_a.at[p, 2 + i], 384)
+    for i in range(4):
+        for p in parts:
+            got = near(p, ORDERS[p][2], 2, i)
+            take(got, recv_b.at[p, 2 + i])
+            tell(p, got)
+
+    for p in parts:
+        third = ORDERS[p][2]
+        for i in range(4):
             take_halves(near(p, third, -1, i), near(p, third, 1, i), send_b.at[p, 2 + i])
     for sem in (sib_send, sib_recv):
         drain(buf.at[pl.ds(0, 3), :, :, pl.ds(0, 672)], sem)
 
 
 def step_kernel(
-    pieces_ref, mom_ref, table_ref, fresh_ref, buf,
-    hits, outgoing, slot_row, slots, got, place, columns, packed, terms, partial, terms2, summed, relay, chosen, arrived, mcol,
+    rows_ref, mom_ref, table_ref, fresh_ref, buf,
+    wide, pieces, hits, outgoing, slot_row, slots, got, place, columns, packed, terms, partial, terms2, summed, relay, chosen, arrived, mcol,
     gram, gram2, ga, gb, pbs, ta, xa,
     a2a_send, a2a_recv, swap_send, swap_recv, rs1_send, rs2_send, ag1_send, ag2_send,
     h1_send, h1_recv, h2_send, h2_recv, sib_send, sib_recv, slot_sem,
@@ -357,7 +350,13 @@
     lines = lax.broadcasted_iota(jnp.int32, (16 * DEVICES, DEVICES), 0)
     for i in range(5):
         hits[:, 128 * i : 128 * i + 128] = jnp.where(lines == line + i, 1.0, 0.0).astype(BF16)
-    outgoing[...] = dot(hits[...], pieces_ref[...]).astype(BF16).reshape(DEVICES, 16, 128)
+    wide[...] = jnp.zeros_like(wide)
+    for i in range(9):
+        wide[i, :, 0:56] = rows_ref[i].astype(F32)
+    for i in range(5):
+        pair = wide[2 * i] + pltpu.roll(wide[2 * i + 1], 64, 1)
+        pieces[128 * i : 128 * i + 128, :] = pair.astype(BF16)
+    outgoing[...] = dot(hits[...], pieces[...]).astype(BF16).reshape(DEVICES, 16, 128)
     slot_copy.wait()
     greeted()
 
@@ -594,33 +593,34 @@
     buf[chip // 16, lax.rem(chip // 4, 4), lax.rem(chip, 4), pl.ds(pl.multiple_of(R * core, 16), R)] = (
         value.T[0:R, :].astype(BF16)
     )
-    gather_steps(buf, send_a, send_b, recv_a, recv_b, sib_send, sib_recv)
-
-    drain(others, a2a_send)
-    swap.wait_send()
-    drain(packed.at[pl.ds(0, 1152)], rs1_send)
-    drain(packed.at[pl.ds(0, 360)], rs2_send)
-    drain(packed.at[pl.ds(0, 360)], ag1_send)
-    drain(packed.at[pl.ds(0, 1152)], ag2_send)
-
-    @pl.when(relays)
-    def _():
-        drain(relay.at[pl.ds(0, 3 * (RELAYS - 1))], h1_send)
-
-    @pl.when(jnp.logical_not(relays))
-    def _():
-        drain(relay.at[pl.ds(0, 3 * RELAYS)], h1_send)
-
-    @pl.when(sole)
-    def _():
-        drain(relay.at[pl.ds(0, 3 * TILES)], h2_send)
-
-    @pl.when(spans)
-    def _():
-        drain(relay.at[pl.ds(0, 6 * TILES)], h2_send)
-
-
-def step(pieces, momentum, table):
+    def earlier_sent():
+        drain(others, a2a_send)
+        swap.wait_send()
+        drain(packed.at[pl.ds(0, 1152)], rs1_send)
+        drain(packed.at[pl.ds(0, 360)], rs2_send)
+        drain(packed.at[pl.ds(0, 360)], ag1_send)
+        drain(packed.at[pl.ds(0, 1152)], ag2_send)
+
+        @pl.when(relays)
+        def _():
+            drain(relay.at[pl.ds(0, 3 * (RELAYS - 1))], h1_send)
+
+        @pl.when(jnp.logical_not(relays))
+        def _():
+            drain(relay.at[pl.ds(0, 3 * RELAYS)], h1_send)
+
+        @pl.when(sole)
+        def _():
+            drain(relay.at[pl.ds(0, 3 * TILES)], h2_send)
+
+        @pl.when(spans)
+        def _():
+            drain(relay.at[pl.ds(0, 6 * TILES)], h2_send)
+
+    gather_steps(buf, send_a, send_b, recv_a, recv_b, sib_send, sib_recv, earlier_sent)
+
+
+def step(rows, momentum, table):
     return pl.pallas_call(
         step_kernel,
         out_shape=(
@@ -637,6 +637,8 @@
             pl.BlockSpec(memory_space=pltpu.VMEM),
         ),
         scratch_shapes=[
+            pltpu.VMEM((10, 128, 128), F32),
+            pltpu.VMEM((640, 128), BF16),
             pltpu.VMEM((16 * DEVICES, 5 * 128), BF16),
             pltpu.VMEM((DEVICES, 16, 128), BF16),
             pltpu.VMEM((1, DEVICES), jnp.int32),
@@ -669,7 +671,7 @@
             collective_id=0, has_side_effects=True, vmem_limit_bytes=40 * 2**20
         ),
         name="step",
-    )(pieces, momentum, table)
+    )(rows, momentum, table)
 
 
 def place_kernel(buf, fresh, update, momentum, sem):
@@ -702,9 +704,7 @@
 
 
 def local(grads, momentum, table):
-    pieces = jnp.pad(grads.reshape(9, 128, 56), ((0, 1), (0, 0), (0, 8)))
-    pieces = pieces.reshape(5, 2, 128, 64).transpose(0, 2, 1, 3).reshape(640, 128)
-    fresh, buf = step(pieces, momentum, table.reshape(1, DEVICES))
+    fresh, buf = step(grads.reshape(9, 128, 56), momentum, table.reshape(1, DEVICES))
     return place_results(buf, fresh)
 
 

time: 126 us -> 121 us (0.960)
  Pallas kernels: 122 us -> 118 us
    pallas_call x1, Pallas kernels: 116 us -> 112 us  [step(): pl.pallas_call(step_kernel, out_shape=(pltpu.VMEM(momentum.shape, F32), p...]
    reshape x3 -> x1, local copies, waits for them, and re-layouts: 2.66 us -> 2.2 us  [local(): grads.reshape(9, 128, 56)]
where the time goes in v6:
time: 121 us
  Pallas kernels  118 us (98%)
  local copies, waits for them, and re-layouts  2.2 us (2%)
    pallas_call x1, Pallas kernels, step(): pl.pallas_call(step_kernel, out_shape=(pltpu.VMEM(momentum.shape, F32), p...  112 us
    pallas_call x1, Pallas kernels, place_results(): pl.pallas_call(place_kernel, out_shape=(jax.ShapeDtypeStruct((2 * R, 128...  6.47 us

profile of v6, /device:TPU:1, one launch (start us, length us, event | category | flops | bytes accessed | tf_op | source)
XLA Modules:
  0.0 121.2 jit_solution(10645843075177761230)
XLA Ops:
  0.6 2.2 %reshape.10.rows_ref = bf16[9,128,56]{2,1,0:T(8,128)(2,1)} reshape(bf16[9,7168]{1,0:T(8,128)(2,1)} %param.3) | data formatting | bytes 258048 | tf_op jit(solution)/shard_map/reshape | solution.py:707
  2.8 111.8 %step.1 = (f32[3,56,1152]{2,1,0:T(8,128)S(1)}, bf16[4,4,4,1152,128]{4,3,2,1,0:T(8,128)(2,1)S(1)}) custom-call(bf16[9,128,56]{2,1,0:T(8,128)(2,1)} %reshape.10.rows_ref, f32[3,56,1152]{2,1,0:T(8,128)} %mom_ref.1, s32[1,128]{1,0:T(1,128)} %bitcast.1), custom_call_target="tpu_custom_call" | custom-call | tf_op jit(solution)/shard_map/step/pallas_call | solution.py:624
  114.6 6.5 %place.1 = (bf16[1152,7168]{1,0:T(8,128)(2,1)}, f32[3,56,1152]{2,1,0:T(8,128)}) custom-call(bf16[4,4,4,1152,128]{4,3,2,1,0:T(8,128)(2,1)S(1)} %get-tuple-element.4.buf, f32[3,56,1152]{2,1,0:T(8,128)S(1)} %get-tuple-element.5.fresh), custom_call_target="tpu_custom_call" | custom-call | tf_op jit(solution)/shard_map/place/pallas_call | solution.py:692

commit v7 on v6

--- a/solution.py
+++ b/solution.py
@@ -267,6 +267,11 @@
             pass_on(part, 2 + i, got, d, axis, step)
             tell(part, got)
 
+    def finish(part, i):
+        got = near(part, ORDERS[part][2], 2, i)
+        take(got, recv_b.at[part, 2 + i])
+        tell(part, got)
+
     for p in parts:
         own, axis = tile(p, home), ORDERS[p][0]
         both(p, 0, own, axis)
@@ -304,6 +309,9 @@
     for i in (1, 2, 3):
         for p in parts:
             forward(p, i)
+        if i > 1:
+            for p in parts:
+                finish(p, i - 2)
     for p in parts:
         first, second, third = ORDERS[p]
         take(tile(p, home), send_a.at[p, 0], 576)
@@ -311,11 +319,9 @@
         take_halves(line(p, shift(home, second, -1)), line(p, shift(home, second, 1)), send_b.at[p, 1])
         for i in range(4):
             take(near(p, third, 0, i), send_a.at[p, 2 + i], 384)
-    for i in range(4):
+    for i in (2, 3):
         for p in parts:
-            got = near(p, ORDERS[p][2], 2, i)
-            take(got, recv_b.at[p, 2 + i])
-            tell(p, got)
+            finish(p, i)
 
     for p in parts:
         third = ORDERS[p][2]

time: 121 us -> 121 us (level)
  no operation moved by 1% of the time
where the time goes in v7:
time: 121 us
  Pallas kernels  118 us (98%)
  local copies, waits for them, and re-layouts  2.2 us (2%)
    pallas_call x1, Pallas kernels, step(): pl.pallas_call(step_kernel, out_shape=(pltpu.VMEM(momentum.shape, F32), p...  112 us
    pallas_call x1, Pallas kernels, place_results(): pl.pallas_call(place_kernel, out_shape=(jax.ShapeDtypeStruct((2 * R, 128...  6.47 us

profile of v7, /device:TPU:1, one launch (start us, length us, event | category | flops | bytes accessed | tf_op | source)
XLA Modules:
  0.0 121.2 jit_solution(9393274782919233279)
XLA Ops:
  0.6 2.2 %reshape.10.rows_ref = bf16[9,128,56]{2,1,0:T(8,128)(2,1)} reshape(bf16[9,7168]{1,0:T(8,128)(2,1)} %param.3) | data formatting | bytes 258048 | tf_op jit(solution)/shard_map/reshape | solution.py:713
  2.8 111.8 %step.1 = (f32[3,56,1152]{2,1,0:T(8,128)S(1)}, bf16[4,4,4,1152,128]{4,3,2,1,0:T(8,128)(2,1)S(1)}) custom-call(bf16[9,128,56]{2,1,0:T(8,128)(2,1)} %reshape.10.rows_ref, f32[3,56,1152]{2,1,0:T(8,128)} %mom_ref.1, s32[1,128]{1,0:T(1,128)} %bitcast.1), custom_call_target="tpu_custom_call" | custom-call | tf_op jit(solution)/shard_map/step/pallas_call | solution.py:630
  114.6 6.5 %place.1 = (bf16[1152,7168]{1,0:T(8,128)(2,1)}, f32[3,56,1152]{2,1,0:T(8,128)}) custom-call(bf16[4,4,4,1152,128]{4,3,2,1,0:T(8,128)(2,1)S(1)} %get-tuple-element.4.buf, f32[3,56,1152]{2,1,0:T(8,128)S(1)} %get-tuple-element.5.fresh), custom_call_target="tpu_custom_call" | custom-call | tf_op jit(solution)/shard_map/place/pallas_call | solution.py:698
